TPU v7x, 32 devices: a whole 2x2x4 slice. The times are simulated.
32 devices in a mesh: seq: 8 (over y, x, core), dp: 4 (over z).
Axes of the slice: x: 2, y: 2, z: 4, core: 2. Of those that a mesh axis runs over, the one named last changes fastest.
Arguments:
- q_raw: bfloat16 [4, 1024, 1024], P('dp', 'seq'), may hold values from -21 to 21
- k_raw: bfloat16 [4, 1024, 256], P('dp', 'seq'), may hold values from -21 to 21
- v_raw: bfloat16 [4, 1024, 256], P('dp', 'seq'), may hold values from -6 to 6
- q_gain: float32 [128], P('dp'), may hold values from 0.5 to 6
- k_gain: float32 [128], P('dp'), may hold values from 0.5 to 6
- key_blocks: int32 [8, 8, 6], P('seq'), may hold values from -1 to 7, as said below
- d_context: bfloat16 [4, 1024, 1024], P('dp', 'seq'), may hold values from -21 to 21
Outputs:
- q_raw_grad: bfloat16 [4, 1024, 1024], P('dp', 'seq')
- k_raw_grad: bfloat16 [4, 1024, 256], P('dp', 'seq')
- v_grad: bfloat16 [4, 1024, 256], P('dp', 'seq')
- q_gain_grad: float32 [128], P('dp')
- k_gain_grad: float32 [128], P('dp')
Inputs may be any that keep to these rules, and one draw needn't show every extreme that they name: key_blocks[h, b, 0] = b; slots 1 and 2 hold b - 1 and b + 1, or -1 past the ends of the sequence; the next 1 slots hold blocks 0 to 0; the last 2 slots hold drawn blocks, which may repeat earlier slots.
All inputs are finite; a program needn't handle non-finite values.
Results may differ from a plain program's by a relative error of at most 0.017.
The roundings to bfloat16 on the way count: a program that leaves them out, or rounds other values in their place, can miss the bound.
Values may be sent and summed in bfloat16 or wider, within the bound.
A program may use at most 64 MiB of HBM per device.

v0:
```python
import math

import jax
import jax.numpy as jnp
from jax import lax
from jax.sharding import PartitionSpec as P

BLK = 128
GLOB = 1


EPSILON = 1e-06


def slot_keep(pattern):
    slot_count = pattern.shape[-1]
    present = pattern >= 0
    same_block = pattern[:, :, None] == pattern[:, None, :]
    earlier = jnp.arange(slot_count)[None, :] < jnp.arange(slot_count)[:, None]
    repeated = jnp.any(same_block & earlier[None, :, :], axis=2)
    return present & jnp.logical_not(repeated)


def norm_rows(raw_rows, gain_vec):
    length_total = raw_rows.shape[0]
    width = gain_vec.shape[0]
    values = raw_rows.astype(jnp.float32).reshape(length_total, -1, width)
    inverse = lax.rsqrt(jnp.mean(values * values, axis=-1, keepdims=True) + EPSILON)
    normed = (values * inverse * gain_vec).astype(jnp.bfloat16).reshape(length_total, -1)
    return (normed, inverse)


def norm_back(raw_rows, inverse, gain_vec, d_normed):
    length_total = raw_rows.shape[0]
    width = gain_vec.shape[0]
    values = raw_rows.astype(jnp.float32).reshape(length_total, -1, width)
    upstream = d_normed.astype(jnp.float32).reshape(length_total, -1, width)
    scaled = gain_vec * upstream
    row_total = jnp.sum(scaled * values, axis=-1, keepdims=True)
    d_raw = inverse * scaled - inverse * inverse * inverse * values * row_total / width
    gain_part = jnp.sum(upstream * values * inverse, axis=(0, 1))
    return (d_raw.astype(jnp.bfloat16).reshape(length_total, -1), gain_part)


def softmax_rows(score_matrix, axes):
    row_peak = jnp.max(score_matrix, axis=axes, keepdims=True)
    raised = jnp.exp(score_matrix - row_peak)
    return raised / jnp.sum(raised, axis=axes, keepdims=True)


def tile_layout(head_array):
    length_total, width_per_head = head_array.shape
    return head_array.reshape(length_total // BLK, BLK, width_per_head)


def group_size(blocks):
    return math.gcd(blocks, max(1, 1024 // BLK))


def backward_head(q_head, k_head, v_head, d_head, pattern):
    length_total, width_per_head = q_head.shape
    blocks = length_total // BLK
    lead_rows = GLOB * BLK
    logit_scale = 1.0 / math.sqrt(width_per_head)
    keep_slot = slot_keep(pattern)
    picked = jnp.maximum(pattern, 0)
    query_tiles = tile_layout(q_head)
    k_tiles = tile_layout(k_head)
    v_tiles = tile_layout(v_head)
    tile_gradient = tile_layout(d_head)
    group_len = group_size(blocks)
    top_precision = lax.Precision.HIGHEST

    def one_group(carry, group_index):
        k_acc, v_acc = carry
        first_block = group_index * group_len
        query_rows = lax.dynamic_slice_in_dim(query_tiles, first_block, group_len, 0)
        grad_rows = lax.dynamic_slice_in_dim(tile_gradient, first_block, group_len, 0)
        chosen = lax.dynamic_slice_in_dim(picked, first_block, group_len, 0)
        allowed = lax.dynamic_slice_in_dim(keep_slot, first_block, group_len, 0)
        selected_keys = k_tiles[chosen]
        selected_values = v_tiles[chosen]
        score_matrix = (
            jnp.einsum(
                "gqd,gskd->gqsk", query_rows, selected_keys, preferred_element_type=jnp.float32
            )
            * logit_scale
        )
        score_matrix = jnp.where(allowed[:, None, :, None], score_matrix, -jnp.inf)
        weights = softmax_rows(score_matrix, (2, 3))
        weight_reduced = weights.astype(jnp.bfloat16)
        sparse_query_row = (first_block + jnp.arange(group_len) >= GLOB)[:, None, None, None]
        weight_gradient = jnp.einsum(
            "gqd,gskd->gqsk", grad_rows, selected_values, preferred_element_type=jnp.float32
        )
        row_delta = jnp.sum(weights * weight_gradient, axis=(2, 3), keepdims=True)
        score_gradient = jnp.where(
            sparse_query_row, weights * (weight_gradient - row_delta) * logit_scale, 0.0
        ).astype(jnp.bfloat16)
        d_query = jnp.einsum(
            "gqsk,gskd->gqd", score_gradient, selected_keys, preferred_element_type=jnp.float32
        )
        key_pieces = jnp.einsum(
            "gqsk,gqd->gskd", score_gradient, query_rows, preferred_element_type=jnp.float32
        )
        kept_low = jnp.where(sparse_query_row, weight_reduced, jnp.zeros_like(weight_reduced))
        value_pieces = jnp.einsum(
            "gqsk,gqd->gskd", kept_low, grad_rows, preferred_element_type=jnp.float32
        )
        one_hot = (
            (chosen[:, :, None] == jnp.arange(blocks)[None, None, :]) & allowed[:, :, None]
        ).astype(jnp.float32)
        k_acc = k_acc + jnp.einsum("gsn,gskd->nkd", one_hot, key_pieces, precision=top_precision)
        v_acc = v_acc + jnp.einsum("gsn,gskd->nkd", one_hot, value_pieces, precision=top_precision)
        return ((k_acc, v_acc), d_query)

    zero_acc = jnp.zeros((blocks, BLK, width_per_head), jnp.float32)
    sums, q_groups = lax.scan(one_group, (zero_acc, zero_acc), jnp.arange(blocks // group_len))
    query_sparse = q_groups.reshape(length_total, width_per_head)
    k_sparse = sums[0].reshape(length_total, width_per_head)
    v_sparse = sums[1].reshape(length_total, width_per_head)
    q_lead = q_head[:lead_rows]
    d_lead = d_head[:lead_rows]
    lead_scores = (
        jnp.einsum("qd,kd->qk", q_lead, k_head, preferred_element_type=jnp.float32) * logit_scale
    )
    lead_weights = softmax_rows(lead_scores, (1,))
    lead_low = lead_weights.astype(jnp.bfloat16)
    lead_dprob = jnp.einsum("qd,kd->qk", d_lead, v_head, preferred_element_type=jnp.float32)
    lead_delta = jnp.sum(lead_weights * lead_dprob, axis=1, keepdims=True)
    lead_dscore = (lead_weights * (lead_dprob - lead_delta) * logit_scale).astype(jnp.bfloat16)
    lead_dq = jnp.dot(lead_dscore, k_head, preferred_element_type=jnp.float32)
    lead_dk = jnp.einsum("qk,qd->kd", lead_dscore, q_lead, preferred_element_type=jnp.float32)
    lead_dv = jnp.einsum("qk,qd->kd", lead_low, d_lead, preferred_element_type=jnp.float32)
    d_query = jnp.concatenate([lead_dq, query_sparse[lead_rows:]], axis=0).astype(jnp.bfloat16)
    return (d_query, k_sparse + lead_dk, v_sparse + lead_dv)


def widen_heads(rows, width_per_head, group_len):
    tokens = rows.shape[0]
    kv_count = rows.shape[1] // width_per_head
    spread = jnp.broadcast_to(
        rows.reshape(tokens, kv_count, 1, width_per_head),
        (tokens, kv_count, group_len, width_per_head),
    )
    return spread.reshape(tokens, kv_count * group_len * width_per_head)


def shards(q_raw, k_raw, v_raw, q_gain, k_gain, key_blocks, d_context):
    q_full, k_full = (
        lax.all_gather(q_gain, "dp", axis=0, tiled=True),
        lax.all_gather(k_gain, "dp", axis=0, tiled=True),
    )
    q_normed, q_inverse = norm_rows(q_raw[0], q_full)
    k_normed, k_inverse = norm_rows(k_raw[0], k_full)
    width_per_head = q_full.shape[0]
    group_len = q_raw.shape[2] // k_raw.shape[2]
    tokens = q_raw.shape[1]
    k_wide = widen_heads(k_normed, width_per_head, group_len)
    v_wide = widen_heads(v_raw[0], width_per_head, group_len)
    q_heads, k_heads, v_heads, d_heads = (
        lax.all_to_all(q_normed, "seq", split_axis=1, concat_axis=0, tiled=True),
        lax.all_to_all(k_wide, "seq", split_axis=1, concat_axis=0, tiled=True),
        lax.all_to_all(v_wide, "seq", split_axis=1, concat_axis=0, tiled=True),
        lax.all_to_all(d_context[0], "seq", split_axis=1, concat_axis=0, tiled=True),
    )
    length_total = q_heads.shape[0]
    head_count = key_blocks.shape[0]

    def split_heads(head_array):
        return head_array.reshape(length_total, head_count, width_per_head)

    def merge_heads(head_array):
        return head_array.reshape(length_total, head_count * width_per_head)

    backward = jax.vmap(backward_head, in_axes=(1, 1, 1, 1, 0), out_axes=1)
    dq_heads, dk_heads, dv_heads = backward(
        split_heads(q_heads),
        split_heads(k_heads),
        split_heads(v_heads),
        split_heads(d_heads),
        key_blocks,
    )
    dq_heads = merge_heads(dq_heads)
    dk_heads = merge_heads(dk_heads)
    dv_heads = merge_heads(dv_heads)
    d_q_normed = lax.all_to_all(dq_heads, "seq", split_axis=0, concat_axis=1, tiled=True)
    dk_terms, dv_terms = (
        lax.all_to_all(dk_heads, "seq", split_axis=0, concat_axis=1, tiled=True),
        lax.all_to_all(dv_heads, "seq", split_axis=0, concat_axis=1, tiled=True),
    )
    kv_count = k_raw.shape[2] // width_per_head
    d_k_normed = (
        jnp.sum(dk_terms.reshape(tokens, kv_count, group_len, width_per_head), axis=2)
        .astype(jnp.bfloat16)
        .reshape(tokens, kv_count * width_per_head)
    )
    v_grad = (
        jnp.sum(dv_terms.reshape(tokens, kv_count, group_len, width_per_head), axis=2)
        .astype(jnp.bfloat16)
        .reshape(tokens, kv_count * width_per_head)
    )
    q_grad, q_part = norm_back(q_raw[0], q_inverse, q_full, d_q_normed)
    k_grad, k_part = norm_back(k_raw[0], k_inverse, k_full, d_k_normed)
    q_total, k_total = lax.psum((q_part, k_part), ("seq", "dp"))
    shard_len = q_gain.shape[0]
    offset = lax.axis_index("dp") * shard_len
    q_gain_grad = lax.dynamic_slice_in_dim(q_total, offset, shard_len)
    k_gain_grad = lax.dynamic_slice_in_dim(k_total, offset, shard_len)
    return (q_grad[None], k_grad[None], v_grad[None], q_gain_grad, k_gain_grad)


def solution(mesh):
    placed = (
        P("dp", "seq", None),
        P("dp", "seq", None),
        P("dp", "seq", None),
        P("dp"),
        P("dp"),
        P("seq", None, None),
        P("dp", "seq", None),
    )
    return jax.shard_map(
        shards,
        mesh=mesh,
        in_specs=placed,
        out_specs=(
            P("dp", "seq", None),
            P("dp", "seq", None),
            P("dp", "seq", None),
            P("dp"),
            P("dp"),
        ),
        check_vma=False,
    )
```

profile of v0, /device:TPU:0, one launch (start us, length us, event | category | flops | bytes accessed | tf_op | source)
XLA Modules:
  0.0 154.1 jit_solution(3856394256306446753)
XLA Ops:
  0.7 1.0 copy.100
  1.8 0.6 multiply_multiply_fusion.1
  2.4 1.2 dynamic-slice
  4.3 0.9 dynamic-update-slice.1
  5.2 0.8 dynamic-update-slice
  6.0 13.4 %all-reduce.3 = (f32[128]{0:T(128)S(1)}, f32[128]{0:T(128)S(1)}) all-reduce(f32[128]{0:T(128)S(1)} %dynamic-update-slice.1, f32[128]{0:T(128)S(1)} %dynamic-update-slice), channel_id=1, replica_groups=mesh['seq'=8,'dp'=4] {'dp'}, use_global_device_ids=true, to_apply=%add.1 | all-reduce | flops 256 | bytes 2048
  19.6 0.7 broadcast_in_dim.103
  20.3 3.7 %all-to-all-start.1 = ((bf16[128,8,128]{2,0,1:T(8,128)(2,1)}), bf16[128,8,128]{2,0,1:T(8,128)(2,1)S(1)}, u32[]{:S(2)}, u32[]{:S(2)}) async-start(bf16[128,8,128]{2,0,1:T(8,128)(2,1)} %bitcast.6), calls=%async_computation.1 | async-start | bytes 524288 | tf_op jit(solution)/shard_map/all_to_all | solution.py:163
  24.0 0.8 copy.105
  24.8 0.7 copy.151
  25.5 1.1 copy.98
  26.6 0.1 copy.99
  26.8 0.3 and_reduce_fusion
  27.2 0.6 multiply_multiply_fusion
  27.8 0.9 multiply_convert_fusion.1
  28.9 2.1 %all-to-all-done.1 = bf16[128,8,128]{2,0,1:T(8,128)(2,1)S(1)} async-done(((bf16[128,8,128]{2,0,1:T(8,128)(2,1)}), bf16[128,8,128]{2,0,1:T(8,128)(2,1)S(1)}, u32[]{:S(2)}, u32[]{:S(2)}) %all-to-all-start.1) | async-done | bytes 262176 | tf_op jit(solution)/shard_map/all_to_all | solution.py:163
  31.0 0.7 broadcast_in_dim.105
  31.7 3.4 %all-to-all-start.3 = ((bf16[128,8,128]{2,0,1:T(8,128)(2,1)}), bf16[128,8,128]{2,0,1:T(8,128)(2,1)S(1)}, u32[]{:S(2)}, u32[]{:S(2)}) async-start(bf16[128,8,128]{2,0,1:T(8,128)(2,1)} %bitcast.12), calls=%async_computation.3 | async-start | bytes 524288 | tf_op jit(solution)/shard_map/all_to_all | solution.py:164
  35.2 6.8 %all-to-all-done.3 = bf16[128,8,128]{2,0,1:T(8,128)(2,1)S(1)} async-done(((bf16[128,8,128]{2,0,1:T(8,128)(2,1)}), bf16[128,8,128]{2,0,1:T(8,128)(2,1)S(1)}, u32[]{:S(2)}, u32[]{:S(2)}) %all-to-all-start.3) | async-done | bytes 262176 | tf_op jit(solution)/shard_map/all_to_all | solution.py:164
  42.0 3.4 %all-to-all-start = ((bf16[128,8,128]{2,0,1:T(8,128)(2,1)}), bf16[128,8,128]{2,0,1:T(8,128)(2,1)S(1)}, u32[]{:S(2)}, u32[]{:S(2)}) async-start(bf16[128,8,128]{2,0,1:T(8,128)(2,1)} %multiply_convert_fusion.1), calls=%async_computation | async-start | bytes 524288 | tf_op jit(solution)/shard_map/all_to_all | solution.py:162
  45.4 0.5 iota_compare_fusion.2
  46.1 0.2 copy.102
  46.3 0.9 copy.103
  47.2 0.7 copy.119
  47.9 0.6 broadcast_bitcast_fusion
  48.5 2.0 %gather_fusion = bf16[48,128,128]{2,1,0:T(8,128)(2,1)} fusion(bf16[1,8,128,128]{3,2,1,0:T(8,128)(2,1)S(1)} %bitcast.176, s32[48]{0:T(128)S(1)} %reshape.471), kind=kCustom, calls=%fused_computation | custom fusion | bytes 3146112 | tf_op jit(solution)/shard_map/vmap()/while/body/eval_jaxpr/gather | solution.py:81
  50.5 2.0 %gather_fusion.1 = bf16[48,128,128]{2,1,0:T(8,128)(2,1)} fusion(bf16[1,8,128,128]{3,2,1,0:T(8,128)(2,1)S(1)} %bitcast.181, s32[48]{0:T(128)S(1)} %reshape.471), kind=kCustom, calls=%fused_computation.1 | custom fusion | bytes 3146112 | tf_op jit(solution)/shard_map/vmap()/while/body/eval_jaxpr/gather | solution.py:82
  52.5 4.1 %all-to-all-start.2 = ((bf16[128,8,128]{2,0,1:T(8,128)(2,1)}), bf16[128,8,128]{2,0,1:T(8,128)(2,1)}, u32[]{:S(2)}, u32[]{:S(2)}) async-start(bf16[128,8,128]{2,0,1:T(8,128)(2,1)} %copy.103), calls=%async_computation.2 | async-start | bytes 524288 | tf_op jit(solution)/shard_map/all_to_all | solution.py:165
  56.6 2.1 %fusion.10 = (f32[8,128]{1,0:T(8,128)S(1)}, f32[8,128,6,128]{1,3,2,0:T(8,128)S(1)}) fusion(pred[8,6]{1,0:T(8,128)(4,1)S(1)} %fusion.59, bf16[8,6,128,128]{3,2,1,0:T(8,128)(2,1)} %bitcast.179, bf16[128,8,128]{2,0,1:T(8,128)(2,1)} %copy-done.8), kind=kOutput, calls=%fused_computation.16 | convolution fusion | flops 203684864 | bytes 4984880 | tf_op jit(solution)/shard_map/vmap()/while/body/eval_jaxpr/gqd,gskd->gqsk/dot_general | solution.py:84
  58.7 1.3 fusion.12
  60.1 3.6 %all-to-all-done.2 = bf16[128,8,128]{2,0,1:T(8,128)(2,1)} async-done(((bf16[128,8,128]{2,0,1:T(8,128)(2,1)}), bf16[128,8,128]{2,0,1:T(8,128)(2,1)}, u32[]{:S(2)}, u32[]{:S(2)}) %all-to-all-start.2) | async-done | bytes 262176 | tf_op jit(solution)/shard_map/all_to_all | solution.py:165
  63.7 2.6 %fusion.1 = (f32[8,128]{1,0:T(8,128)S(1)}, f32[8,6,128,128]{3,2,1,0:T(8,128)S(1)}) fusion(f32[8,128]{1,0:T(8,128)} %fusion.12, f32[8,128]{1,0:T(8,128)S(1)} %get-tuple-element.67, f32[8,128,6,128]{1,3,2,0:T(8,128)S(1)} %get-tuple-element.68, pred[8,6]{1,0:T(8,128)(4,1)S(1)} %fusion.59, bf16[8,6,128,128]{3,2,1,0:T(8,128)(2,1)} %bitcast.188, ...), kind=kOutput, calls=%fused_computation.5 | convolution fusion | flops 206044160 | bytes 8138800 | tf_op jit(solution)/shard_map/vmap()/while/body/eval_jaxpr/gqd,gskd->gqsk/dot_general | solution.py:93
  66.3 1.4 fusion.5
  67.7 0.6 fusion.27
  68.4 1.1 fusion.68
  69.5 0.2 fusion.34
  69.7 1.1 multiply_reduce_fusion
  70.8 0.2 multiply_convert_fusion
  71.0 0.2 convolution_convert_fusion
  71.3 0.7 pad_maximum_fusion
  72.0 3.6 %all-to-all-start.4 = ((bf16[8,128,128]{2,1,0:T(8,128)(2,1)}), bf16[8,128,128]{2,1,0:T(8,128)(2,1)S(1)}, u32[]{:S(2)}, u32[]{:S(2)}) async-start(bf16[8,128,128]{2,1,0:T(8,128)(2,1)} %bitcast.34), calls=%async_computation.4 | async-start | bytes 524288 | tf_op jit(solution)/shard_map/all_to_all | solution.py:187
  75.6 2.0 %fusion.40 = f32[8,6,128,128]{3,2,1,0:T(8,128)S(1)} fusion(bf16[8,128,6,128]{1,3,2,0:T(8,128)(2,1)} %copy-done, bf16[128,8,128]{2,0,1:T(8,128)(2,1)} %copy-done.8), kind=kOutput, calls=%fused_computation.56 | convolution fusion | flops 201326592 | bytes 4980736 | tf_op jit(solution)/shard_map/vmap()/while/body/eval_jaxpr/gqsk,gqd->gskd/dot_general | solution.py:103
  77.6 4.4 %fusion.17 = f32[8,128,128]{2,0,1:T(8,128)S(1)} fusion(f32[8,6,128,128]{3,2,1,0:T(8,128)S(1)} %fusion.40, s32[8,6]{0,1:T(8,128)S(1)} %copy.118, pred[8,6]{0,1:T(8,128)(4,1)} %copy.119), kind=kOutput, calls=%fused_computation.23 | convolution fusion | flops 75498240 | bytes 3670256 | tf_op jit(solution)/shard_map/vmap()/while/body/eval_jaxpr/gsn,gskd->nkd/dot_general | solution.py:113
  82.2 3.5 %fusion.13 = f32[8,6,128,128]{3,2,1,0:T(8,128)} fusion(pred[8]{0:T(512)(128)(4,1)S(1)} %copy-done.31, bf16[128,8,128]{2,0,1:T(8,128)(2,1)} %all-to-all-done.2, f32[8,128,6,128]{1,3,2,0:T(8,128)S(1)} %get-tuple-element.68, f32[8,128]{1,0:T(8,128)S(1)} %copy-done.18, f32[8,128]{1,0:T(8,128)S(1)} %get-tuple-element.67, pred[8,6]{1,0:T(8,128)(4,1)S(1)} %fusion.59), kind=kOutput, calls=%fused_computation.19 | convolution fusion | flops 206045184 | bytes 6561848 | tf_op jit(solution)/shard_map/vmap()/while/body/eval_jaxpr/gqsk,gqd->gskd/dot_general | solution.py:107
  85.7 1.8 %convolution_add_fusion.1 = f32[1024,128]{1,0:T(8,128)} fusion(f32[1024,128]{1,0:T(8,128)S(1)} %bitcast.187, bf16[128,1024]{1,0:T(8,128)(2,1)S(1)} %copy-done.10, bf16[8,128,128]{2,1,0:T(8,128)(2,1)} %bitcast.184), kind=kOutput, calls=%fused_computation.26 | convolution fusion | flops 33685504 | bytes 1343488 | tf_op jit(solution)/shard_map/vmap(qk,qd->kd)/dot_general | solution.py:133
  87.6 0.7 copy-done.13
  88.3 3.9 %all-to-all-start.5 = ((f32[8,128,128]{2,1,0:T(8,128)}), f32[8,128,128]{2,1,0:T(8,128)S(1)}, u32[]{:S(2)}, u32[]{:S(2)}) async-start(f32[8,128,128]{2,1,0:T(8,128)} %bitcast.46), calls=%async_computation.5 | async-start | bytes 1048576 | tf_op jit(solution)/shard_map/all_to_all | solution.py:189
  92.3 5.6 %fusion.20 = f32[8,128,128]{2,0,1:T(8,128)S(1)} fusion(f32[8,6,128,128]{3,2,1,0:T(8,128)} %fusion.13, s32[8,6]{0,1:T(8,128)S(1)} %copy.118, pred[8,6]{0,1:T(8,128)(4,1)} %copy.119), kind=kOutput, calls=%fused_computation.24 | convolution fusion | flops 75498240 | bytes 3670256 | tf_op jit(solution)/shard_map/vmap()/while/body/eval_jaxpr/gsn,gskd->nkd/dot_general | solution.py:114
  98.0 1.9 %convolution_add_fusion = f32[1024,128]{1,0:T(8,128)} fusion(f32[1024,128]{1,0:T(8,128)S(1)} %bitcast.194, bf16[8,128,128]{2,1,0:T(8,128)(2,1)} %bitcast.10, f32[128,1024]{1,0:T(8,128)S(1)} %copy-done.7, f32[128]{0:T(128)S(1)} %copy-done.28, f32[128]{0:T(128)S(1)} %copy-done.22), kind=kOutput, calls=%fused_computation.25 | convolution fusion | flops 34078720 | bytes 1606656 | tf_op jit(solution)/shard_map/vmap(qk,qd->kd)/dot_general | solution.py:134
  99.9 2.1 %all-to-all-done.5 = f32[8,128,128]{2,1,0:T(8,128)S(1)} async-done(((f32[8,128,128]{2,1,0:T(8,128)}), f32[8,128,128]{2,1,0:T(8,128)S(1)}, u32[]{:S(2)}, u32[]{:S(2)}) %all-to-all-start.5) | async-done | bytes 524320 | tf_op jit(solution)/shard_map/all_to_all | solution.py:189
  102.0 3.5 %all-to-all-start.6 = ((f32[8,128,128]{2,1,0:T(8,128)}), f32[8,128,128]{2,1,0:T(8,128)S(1)}, u32[]{:S(2)}, u32[]{:S(2)}) async-start(f32[8,128,128]{2,1,0:T(8,128)} %bitcast.57), calls=%async_computation.6 | async-start | bytes 1048576 | tf_op jit(solution)/shard_map/all_to_all | solution.py:190
  105.5 2.0 %fusion.26 = bf16[128,8,128]{2,0,1:T(8,128)(2,1)S(1)} fusion(bf16[8,128,128]{2,1,0:T(8,128)(2,1)S(1)} %copy-done.14, f32[128,8,128]{2,0,1:T(8,128)S(1)} %copy-done.5, f32[128,8]{0,1:T(8,128)S(1)} %copy-done.24, f32[128]{0:T(128)S(1)} %copy-done.33, f32[128,8]{0,1:T(8,128)S(1)} %get-tuple-element.64), kind=kOutput, calls=%fused_computation.32 | output fusion | flops 1442943 | bytes 1057280 | tf_op jit(solution)/shard_map/mul | solution.py:40
  107.5 0.2 copy.116
  107.7 0.9 copy.128
  108.5 0.2 fusion.32
  108.9 0.1 multiply_reduce_fusion.2
  109.1 0.2 fusion.48
  109.2 0.7 copy.129
  110.0 5.2 %all-to-all-done.6 = f32[8,128,128]{2,1,0:T(8,128)S(1)} async-done(((f32[8,128,128]{2,1,0:T(8,128)}), f32[8,128,128]{2,1,0:T(8,128)S(1)}, u32[]{:S(2)}, u32[]{:S(2)}) %all-to-all-start.6) | async-done | bytes 524320 | tf_op jit(solution)/shard_map/all_to_all | solution.py:190
  115.2 0.1 copy.126
  115.3 0.7 copy.130
  116.1 36.8 %all-reduce.2 = (f32[128]{0:T(128)S(1)}, f32[128]{0:T(128)S(1)}) all-reduce(f32[128]{0:T(128)S(1)} %fusion.32, f32[128]{0:T(128)S(1)} %bitcast_reduce_fusion.2), channel_id=1, replica_groups=mesh['seq'=8,'dp'=4] {'seq','dp'}, use_global_device_ids=true, to_apply=%region_14.15 | all-reduce | flops 256 | bytes 2048 | tf_op jit(solution)/shard_map/psum | solution.py:205
  152.9 0.6 dynamic_slice.9
  153.5 0.6 dynamic_slice.10
  (96 shorter events, 1.4 us)
Async XLA Ops:
  0.6 28.2 %copy-start.16 = (bf16[1,128,256]{2,1,0:T(8,128)(2,1)S(1)}, bf16[1,128,256]{2,1,0:T(8,128)(2,1)}, u32[]{:S(2)}) copy-start(bf16[1,128,256]{2,1,0:T(8,128)(2,1)} %param.9) | copy-start | bytes 196612
  0.6 45.4 %copy-start.15 = (bf16[1,128,1024]{2,1,0:T(8,128)(2,1)S(1)}, bf16[1,128,1024]{2,1,0:T(8,128)(2,1)}, u32[]{:S(2)}) copy-start(bf16[1,128,1024]{2,1,0:T(8,128)(2,1)} %param.13) | copy-start | bytes 786436
  1.7 18.6 %copy-start.11 = (bf16[1,128,256]{1,2,0:T(8,128)(2,1)}, bf16[1,128,256]{1,2,0:T(8,128)(2,1)S(1)}, u32[]{:S(2)}) copy-start(bf16[1,128,256]{1,2,0:T(8,128)(2,1)S(1)} %copy.100) | copy-start | bytes 196612
  2.4 17.9 %copy-start.19 = (f32[128,2]{0,1:T(2,128)}, f32[128,2]{0,1:T(2,128)S(1)}, u32[]{:S(2)}) copy-start(f32[128,2]{0,1:T(2,128)S(1)} %get-tuple-element.66) | copy-start | bytes 3076
  19.4 31.1 %copy-start.25 = (f32[128]{0:T(128)}, f32[128]{0:T(128)S(1)}, u32[]{:S(2)}) copy-start(f32[128]{0:T(128)S(1)} %get-tuple-element.57) | copy-start | bytes 1540
  19.4 31.1 %copy-start.32 = (f32[128]{0:T(128)}, f32[128]{0:T(128)S(1)}, u32[]{:S(2)}) copy-start(f32[128]{0:T(128)S(1)} %get-tuple-element.58) | copy-start | bytes 1540
  20.3 10.7 %all-to-all-start.1 = ((bf16[128,8,128]{2,0,1:T(8,128)(2,1)}), bf16[128,8,128]{2,0,1:T(8,128)(2,1)S(1)}, u32[]{:S(2)}, u32[]{:S(2)}) async-start(bf16[128,8,128]{2,0,1:T(8,128)(2,1)} %bitcast.6), calls=%async_computation.1 | async-start | bytes 524288 | tf_op jit(solution)/shard_map/all_to_all | solution.py:163
  26.8 4.9 %copy-start.4 = (f32[128,8,128]{2,0,1:T(8,128)}, f32[128,8,128]{2,0,1:T(8,128)S(1)}, u32[]{:S(2)}) copy-start(f32[128,8,128]{2,0,1:T(8,128)S(1)} %copy.99) | copy-start | bytes 1572868
  31.7 10.3 %all-to-all-start.3 = ((bf16[128,8,128]{2,0,1:T(8,128)(2,1)}), bf16[128,8,128]{2,0,1:T(8,128)(2,1)S(1)}, u32[]{:S(2)}, u32[]{:S(2)}) async-start(bf16[128,8,128]{2,0,1:T(8,128)(2,1)} %bitcast.12), calls=%async_computation.3 | async-start | bytes 524288 | tf_op jit(solution)/shard_map/all_to_all | solution.py:164
  42.0 10.5 %copy-start.2 = (bf16[128,8,128]{2,0,1:T(8,128)(2,1)}, bf16[128,8,128]{2,0,1:T(8,128)(2,1)S(1)}, u32[]{:S(2)}) copy-start(bf16[128,8,128]{2,0,1:T(8,128)(2,1)S(1)} %all-to-all-done.3) | copy-start | bytes 786436
  42.0 10.5 %all-to-all-start = ((bf16[128,8,128]{2,0,1:T(8,128)(2,1)}), bf16[128,8,128]{2,0,1:T(8,128)(2,1)S(1)}, u32[]{:S(2)}, u32[]{:S(2)}) async-start(bf16[128,8,128]{2,0,1:T(8,128)(2,1)} %multiply_convert_fusion.1), calls=%async_computation | async-start | bytes 524288 | tf_op jit(solution)/shard_map/all_to_all | solution.py:162
  52.5 4.1 %copy-start.8 = (bf16[128,8,128]{2,0,1:T(8,128)(2,1)}, bf16[128,8,128]{2,0,1:T(8,128)(2,1)S(1)}, u32[]{:S(2)}) copy-start(bf16[128,8,128]{2,0,1:T(8,128)(2,1)S(1)} %all-to-all-done) | copy-start | bytes 786436
  52.5 11.2 %all-to-all-start.2 = ((bf16[128,8,128]{2,0,1:T(8,128)(2,1)}), bf16[128,8,128]{2,0,1:T(8,128)(2,1)}, u32[]{:S(2)}, u32[]{:S(2)}) async-start(bf16[128,8,128]{2,0,1:T(8,128)(2,1)} %copy.103), calls=%async_computation.2 | async-start | bytes 524288 | tf_op jit(solution)/shard_map/all_to_all | solution.py:165
  63.7 2.6 %copy-start.17 = (f32[8,128]{1,0:T(8,128)S(1)}, f32[8,128]{1,0:T(8,128)}, u32[]{:S(2)}) copy-start(f32[8,128]{1,0:T(8,128)} %fusion.12) | copy-start | bytes 12292
  63.7 2.6 %copy-start.30 = (pred[8]{0:T(512)(128)(4,1)S(1)}, pred[8]{0:T(512)(128)(4,1)}, u32[]{:S(2)}) copy-start(pred[8]{0:T(512)(128)(4,1)} %iota_compare_fusion.2) | copy-start | bytes 28
  66.3 1.4 copy-start.1
  67.7 3.1 %copy-start = (bf16[8,128,6,128]{1,3,2,0:T(8,128)(2,1)}, bf16[8,128,6,128]{1,3,2,0:T(8,128)(2,1)S(1)}, u32[]{:S(2)}) copy-start(bf16[8,128,6,128]{1,3,2,0:T(8,128)(2,1)S(1)} %fusion.5) | copy-start | bytes 4718596
  67.7 2.0 %copy-start.3 = (bf16[128,8,128]{2,0,1:T(8,128)(2,1)S(1)}, bf16[128,8,128]{2,0,1:T(8,128)(2,1)}, u32[]{:S(2)}) copy-start(bf16[128,8,128]{2,0,1:T(8,128)(2,1)} %copy-done.2) | copy-start | bytes 786436
  69.4 1.8 %copy-start.6 = (f32[128,1024]{1,0:T(8,128)}, f32[128,1024]{1,0:T(8,128)S(1)}, u32[]{:S(2)}) copy-start(f32[128,1024]{1,0:T(8,128)S(1)} %get-tuple-element.72) | copy-start | bytes 1572868
  69.5 2.6 %copy-start.21 = (f32[128]{0:T(128)}, f32[128]{0:T(128)S(1)}, u32[]{:S(2)}) copy-start(f32[128]{0:T(128)S(1)} %get-tuple-element.71) | copy-start | bytes 1540
  69.7 2.3 %copy-start.27 = (f32[128]{0:T(128)}, f32[128]{0:T(128)S(1)}, u32[]{:S(2)}) copy-start(f32[128]{0:T(128)S(1)} %fusion.34) | copy-start | bytes 1540
  71.0 1.0 copy-start.9
  72.0 15.5 %all-to-all-start.4 = ((bf16[8,128,128]{2,1,0:T(8,128)(2,1)}), bf16[8,128,128]{2,1,0:T(8,128)(2,1)S(1)}, u32[]{:S(2)}, u32[]{:S(2)}) async-start(bf16[8,128,128]{2,1,0:T(8,128)(2,1)} %bitcast.34), calls=%async_computation.4 | async-start | bytes 524288 | tf_op jit(solution)/shard_map/all_to_all | solution.py:187
  77.6 4.6 %copy-start.18 = (f32[8,128]{1,0:T(8,128)S(1)}, f32[8,128]{1,0:T(8,128)}, u32[]{:S(2)}) copy-start(f32[8,128]{1,0:T(8,128)} %fusion.12) | copy-start | bytes 12292
  77.6 4.6 %copy-start.31 = (pred[8]{0:T(512)(128)(4,1)S(1)}, pred[8]{0:T(512)(128)(4,1)}, u32[]{:S(2)}) copy-start(pred[8]{0:T(512)(128)(4,1)} %iota_compare_fusion.2) | copy-start | bytes 28
  82.2 3.5 %copy-start.10 = (bf16[128,1024]{1,0:T(8,128)(2,1)S(1)}, bf16[128,1024]{1,0:T(8,128)(2,1)}, u32[]{:S(2)}) copy-start(bf16[128,1024]{1,0:T(8,128)(2,1)} %copy-done.9) | copy-start | bytes 786436
  87.6 10.4 %copy-start.7 = (f32[128,1024]{1,0:T(8,128)S(1)}, f32[128,1024]{1,0:T(8,128)}, u32[]{:S(2)}) copy-start(f32[128,1024]{1,0:T(8,128)} %copy-done.6) | copy-start | bytes 1572868
  87.6 10.4 %copy-start.22 = (f32[128]{0:T(128)S(1)}, f32[128]{0:T(128)}, u32[]{:S(2)}) copy-start(f32[128]{0:T(128)} %copy-done.21) | copy-start | bytes 1540
  87.6 10.4 %copy-start.28 = (f32[128]{0:T(128)S(1)}, f32[128]{0:T(128)}, u32[]{:S(2)}) copy-start(f32[128]{0:T(128)} %copy-done.27) | copy-start | bytes 1540
  87.6 0.7 copy-start.13
  88.3 13.7 %all-to-all-start.5 = ((f32[8,128,128]{2,1,0:T(8,128)}), f32[8,128,128]{2,1,0:T(8,128)S(1)}, u32[]{:S(2)}, u32[]{:S(2)}) async-start(f32[8,128,128]{2,1,0:T(8,128)} %bitcast.46), calls=%async_computation.5 | async-start | bytes 1048576 | tf_op jit(solution)/shard_map/all_to_all | solution.py:189
  92.2 13.2 %copy-start.5 = (f32[128,8,128]{2,0,1:T(8,128)S(1)}, f32[128,8,128]{2,0,1:T(8,128)}, u32[]{:S(2)}) copy-start(f32[128,8,128]{2,0,1:T(8,128)} %copy-done.4) | copy-start | bytes 1572868
  92.2 13.3 %copy-start.14 = (bf16[8,128,128]{2,1,0:T(8,128)(2,1)S(1)}, bf16[8,128,128]{2,1,0:T(8,128)(2,1)}, u32[]{:S(2)}) copy-start(bf16[8,128,128]{2,1,0:T(8,128)(2,1)} %copy-done.13) | copy-start | bytes 786436
  92.3 13.3 %copy-start.24 = (f32[128,8]{0,1:T(8,128)S(1)}, f32[128,8]{0,1:T(8,128)}, u32[]{:S(2)}) copy-start(f32[128,8]{0,1:T(8,128)} %get-tuple-element.63) | copy-start | bytes 12292
  92.3 13.2 %copy-start.33 = (f32[128]{0:T(128)S(1)}, f32[128]{0:T(128)}, u32[]{:S(2)}) copy-start(f32[128]{0:T(128)} %copy-done.32) | copy-start | bytes 1540
  99.9 9.0 %copy-start.26 = (f32[128]{0:T(128)S(1)}, f32[128]{0:T(128)}, u32[]{:S(2)}) copy-start(f32[128]{0:T(128)} %copy-done.25) | copy-start | bytes 1540
  99.9 9.1 %copy-start.12 = (bf16[1,128,256]{1,2,0:T(8,128)(2,1)S(1)}, bf16[1,128,256]{1,2,0:T(8,128)(2,1)}, u32[]{:S(2)}) copy-start(bf16[1,128,256]{1,2,0:T(8,128)(2,1)} %copy-done.11) | copy-start | bytes 196612
  99.9 9.1 %copy-start.20 = (f32[128,2]{0,1:T(2,128)S(1)}, f32[128,2]{0,1:T(2,128)}, u32[]{:S(2)}) copy-start(f32[128,2]{0,1:T(2,128)} %copy-done.19) | copy-start | bytes 3076
  99.9 9.1 %copy-start.23 = (f32[128,2]{0,1:T(2,128)S(1)}, f32[128,2]{0,1:T(2,128)}, u32[]{:S(2)}) copy-start(f32[128,2]{0,1:T(2,128)} %get-tuple-element.65) | copy-start | bytes 3076
  99.9 9.1 %copy-start.29 = (f32[256]{0:T(256)S(1)}, f32[256]{0:T(256)}, u32[]{:S(2)}) copy-start(f32[256]{0:T(256)} %broadcast_bitcast_fusion) | copy-start | bytes 3076
  102.0 13.2 %all-to-all-start.6 = ((f32[8,128,128]{2,1,0:T(8,128)}), f32[8,128,128]{2,1,0:T(8,128)S(1)}, u32[]{:S(2)}, u32[]{:S(2)}) async-start(f32[8,128,128]{2,1,0:T(8,128)} %bitcast.57), calls=%async_computation.6 | async-start | bytes 1048576 | tf_op jit(solution)/shard_map/all_to_all | solution.py:190
where the time goes:
time: 156 us; the launch traced here: 154 us
  blocking collectives  50.2 us (32%)
  matrix products  26.9 us (17%)
  starting transfers between devices  25.7 us (16%)
  local copies, waits for them, and re-layouts  20 us (13%)
  waiting for transfers between devices  19.8 us (13%)
  other arithmetic  9.61 us (6%)
  between operations  1.9 us (1%)
    psum x1, blocking collectives, shards(): q_total, k_total = lax.psum((q_part, k_part), ('seq', 'dp'))  36.8 us
    unnamed x1, blocking collectives  13.4 us
    unnamed x80, local copies, waits for them, and re-layouts  9.17 us
    all_to_all x1, waiting for transfers between devices, shards(): lax.all_to_all(v_wide, 'seq', split_axis=1, concat_axis=0, tiled=True)  6.83 us
    dot_general x1, matrix products, one_group(): jnp.einsum('gsn,gskd->nkd', one_hot, value_pieces, precision=top_precision)  5.58 us
    all_to_all x1, waiting for transfers between devices, shards(): lax.all_to_all(dv_heads, 'seq', split_axis=0, concat_axis=1, tiled=True)  5.18 us
    dot_general x1, matrix products, one_group(): jnp.einsum('gsn,gskd->nkd', one_hot, key_pieces, precision=top_precision)  4.43 us
    all_to_all x1, starting transfers between devices, shards(): lax.all_to_all(d_context[0], 'seq', split_axis=1, concat_axis=0, tiled=True)  4.14 us
  transfers between devices with their start and end apart: 7, of which 5 were waited for; matrix products, arithmetic and copies ran while one was open for 25% of the time, Pallas kernels for 0%

commit v1 on v0

--- a/solution.py
+++ b/solution.py
@@ -1,8 +1,11 @@
+import functools
 import math
 
 import jax
 import jax.numpy as jnp
 from jax import lax
+from jax.experimental import pallas as pl
+from jax.experimental.pallas import tpu as pltpu
 from jax.sharding import PartitionSpec as P
 
 BLK = 128
@@ -146,7 +149,7 @@
     return spread.reshape(tokens, kv_count * group_len * width_per_head)
 
 
-def shards(q_raw, k_raw, v_raw, q_gain, k_gain, key_blocks, d_context):
+def shards_by_head(q_raw, k_raw, v_raw, q_gain, k_gain, key_blocks, d_context):
     q_full, k_full = (
         lax.all_gather(q_gain, "dp", axis=0, tiled=True),
         lax.all_gather(k_gain, "dp", axis=0, tiled=True),
@@ -210,6 +213,352 @@
     return (q_grad[None], k_grad[None], v_grad[None], q_gain_grad, k_gain_grad)
 
 
+F32 = jnp.float32
+BF16 = jnp.bfloat16
+MESH = pl.DeviceIdType.MESH
+VMEM_ROOM = 56 * 1024 * 1024
+
+
+def token_kernel(
+    n, dpn,
+    q_in, k_in, v_in, gq_in, gk_in, kb_in, d_in,
+    q_out, k_out, v_out, gq_out, gk_out,
+    q_s, d_s, k_all, v_all, kb_all, kbm, gq_all, gk_all, bias,
+    q_hat, q_inv, q_st, q_tr, d_st, d_tr, k_hat, k_tr,
+    s_scr, p_scr, ds_scr, acc, sib_out, sib_in, chip_out, chip_in,
+    q_res, part1, part2,
+    loc, k_snd, k_rcv, v_snd, v_rcv, kf_snd, kf_rcv, vf_snd, vf_rcv,
+    b_snd, b_rcv, gq_snd, gq_rcv, gk_snd, gk_rcv,
+    s_snd, s_rcv, x_snd, x_rcv, p1_snd, p1_rcv, p2_snd, p2_rcv,
+):
+    nc = n // 2
+    hd = q_hat.shape[2]
+    tokens = q_s.shape[0]
+    heads = q_s.shape[1] // hd
+    groups = k_in.shape[1] // hd
+    per = heads // groups
+    wide = per * tokens
+    scale = 1.0 / math.sqrt(hd)
+    raise_by = scale * math.log2(math.e)
+
+    me = lax.axis_index("seq")
+    md = lax.axis_index("dp")
+    core = lax.rem(me, 2)
+    chip = lax.div(me, 2)
+    sib = 2 * chip + 1 - core
+
+    def src_chip(t):
+        return lax.rem(chip + nc - t, nc)
+
+    def dst_chip(t):
+        return lax.rem(chip + t, nc)
+
+    def send(src, dst, snd, rcv, **where):
+        return pltpu.make_async_remote_copy(
+            src_ref=src, dst_ref=dst, send_sem=snd, recv_sem=rcv,
+            device_id=where, device_id_type=MESH,
+        )
+
+    def local(src, dst, i):
+        copy = pltpu.make_async_copy(src, dst, loc.at[i])
+        copy.start()
+        return copy
+
+    own_k = local(k_in, k_all.at[me], 0)
+    own_v = local(v_in, v_all.at[me], 1)
+    own_gq = local(gq_in, gq_all.at[md], 2)
+    own_gk = local(gk_in, gk_all.at[md], 3)
+    own_kb = local(kb_in, kb_all.at[me], 4)
+    own_q = local(q_in, q_s, 5)
+    own_d = local(d_in, d_s, 6)
+
+    barrier = pltpu.get_barrier_semaphore()
+    for r in range(1, n):
+        pl.semaphore_signal(barrier, inc=1, device_id={"seq": lax.rem(me + r, n)}, device_id_type=MESH)
+    for r in range(1, dpn):
+        pl.semaphore_signal(barrier, inc=1, device_id={"dp": lax.rem(md + r, dpn)}, device_id_type=MESH)
+    pl.semaphore_wait(barrier, n - 1 + dpn - 1)
+
+    pending = []
+
+    def go(copy):
+        copy.start()
+        pending.append(copy)
+
+    for r in range(1, dpn):
+        to = lax.rem(md + r, dpn)
+        go(send(gq_in, gq_all.at[md], gq_snd.at[r], gq_rcv.at[r], dp=to))
+        go(send(gk_in, gk_all.at[md], gk_snd.at[r], gk_rcv.at[r], dp=to))
+    for t in range(1, nc):
+        go(send(k_in, k_all.at[me], k_snd.at[t], k_rcv.at[t], seq=2 * dst_chip(t) + core))
+    go(send(k_in, k_all.at[me], k_snd.at[0], k_rcv.at[0], seq=sib))
+    for t in range(1, nc):
+        go(send(v_in, v_all.at[me], v_snd.at[t], v_rcv.at[t], seq=2 * dst_chip(t) + core))
+    go(send(v_in, v_all.at[me], v_snd.at[0], v_rcv.at[0], seq=sib))
+    for r in range(1, n):
+        go(send(kb_in, kb_all.at[me], b_snd.at[r], b_rcv.at[r], seq=lax.rem(me + r, n)))
+
+    def arrived(ref, snd, rcv):
+        send(ref, ref, snd, rcv, seq=sib).wait_recv()
+
+    own_d.wait()
+    for h in range(heads):
+        g, i = h // per, h % per
+        rows = slice(i * tokens, (i + 1) * tokens)
+        x = d_s[:, h * hd:(h + 1) * hd]
+        d_st[g, rows, :] = x
+        d_tr[g, :, rows] = x.astype(F32).T.astype(BF16)
+    own_q.wait()
+    own_gq.wait()
+    own_gk.wait()
+    for r in range(1, dpn):
+        frm = lax.rem(md + dpn - r, dpn)
+        arrived(gq_all.at[frm], gq_snd.at[r], gq_rcv.at[r])
+        arrived(gk_all.at[frm], gk_snd.at[r], gk_rcv.at[r])
+    q_gain = jnp.concatenate([gq_all[i] for i in range(dpn)], axis=1)
+    k_gain = jnp.concatenate([gk_all[i] for i in range(dpn)], axis=1)
+    for h in range(heads):
+        g, i = h // per, h % per
+        rows = slice(i * tokens, (i + 1) * tokens)
+        x = q_s[:, h * hd:(h + 1) * hd].astype(F32)
+        inv = lax.rsqrt(jnp.mean(x * x, axis=1, keepdims=True) + EPSILON)
+        inv = jnp.broadcast_to(inv, (tokens, hd))
+        x = x * inv
+        q_inv[h] = inv
+        q_hat[h] = x
+        x = x * q_gain
+        q_st[g, rows, :] = x.astype(BF16)
+        q_tr[g, :, rows] = x.T.astype(BF16)
+
+    own_kb.wait()
+    for r in range(1, n):
+        arrived(kb_all.at[lax.rem(me + n - r, n)], b_snd.at[r], b_rcv.at[r])
+    held = kb_all.shape[1]
+    for h in range(heads):
+        kbm[h:h + 1, :] = kb_all[h // held, h % held, pl.ds(me, 1), :]
+    named = kbm[...]
+    for j in range(n):
+        hit = jnp.where((named == j) | (me < GLOB), 0.0, -jnp.inf)
+        bias[j] = jnp.broadcast_to(jnp.max(hit, axis=1, keepdims=True), (heads, tokens))
+
+    def forward(t):
+        frm = 2 * src_chip(t) + core
+        arrived(k_all.at[frm], k_snd.at[t], k_rcv.at[t])
+        go(send(k_all.at[frm], k_all.at[frm], kf_snd.at[t], kf_rcv.at[t], seq=sib))
+        arrived(v_all.at[frm], v_snd.at[t], v_rcv.at[t])
+        go(send(v_all.at[frm], v_all.at[frm], vf_snd.at[t], vf_rcv.at[t], seq=sib))
+
+    peak = [jnp.full((1, wide), -jnp.inf, F32) for _ in range(groups)]
+
+    def pair(t):
+        at = src_chip(t)
+        if t == 0:
+            own_k.wait()
+            arrived(k_all.at[sib], k_snd.at[0], k_rcv.at[0])
+        else:
+            arrived(k_all.at[2 * at + 1 - core], kf_snd.at[t], kf_rcv.at[t])
+        keys = k_all[pl.ds(2 * at, 2)].reshape(2 * tokens, groups * hd)
+        for g in range(groups):
+            x = keys[:, g * hd:(g + 1) * hd].astype(F32)
+            inv = lax.rsqrt(jnp.mean(x * x, axis=1, keepdims=True) + EPSILON)
+            x = x * inv
+            k_hat[t, g] = x
+            x = x * k_gain
+            k_tr[t, g] = x.T.astype(BF16)
+            s = jnp.dot(x.astype(BF16), q_tr[g], preferred_element_type=F32)
+            for i in range(2):
+                block = bias[2 * at + i]
+                line = jnp.concatenate([block[h:h + 1] for h in range(g * per, (g + 1) * per)], axis=1)
+                part = s[i * tokens:(i + 1) * tokens] + line
+                s_scr[t, g, i * tokens:(i + 1) * tokens, :] = part
+                peak[g] = jnp.maximum(peak[g], jnp.max(part, axis=0, keepdims=True))
+        if t == 0:
+            own_v.wait()
+            arrived(v_all.at[sib], v_snd.at[0], v_rcv.at[0])
+        else:
+            arrived(v_all.at[2 * at + 1 - core], vf_snd.at[t], vf_rcv.at[t])
+        vals = v_all[pl.ds(2 * at, 2)].reshape(2 * tokens, groups * hd)
+        for g in range(groups):
+            p_scr[t, g] = jnp.dot(vals[:, g * hd:(g + 1) * hd], d_tr[g], preferred_element_type=F32)
+
+    for t in range(nc):
+        if t + 1 < nc:
+            forward(t + 1)
+        pair(t)
+
+    norm, delta = [], []
+    for g in range(groups):
+        total = jnp.zeros((1, wide), F32)
+        cross = jnp.zeros((1, wide), F32)
+        for t in range(nc):
+            e = jnp.exp2((s_scr[t, g] - peak[g]) * raise_by)
+            s_scr[t, g] = e
+            total = total + jnp.sum(e, axis=0, keepdims=True)
+            cross = cross + jnp.sum(e * p_scr[t, g], axis=0, keepdims=True)
+        inv = 1.0 / total
+        norm.append(inv)
+        delta.append(cross * inv)
+
+    k_part = jnp.zeros((1, hd), F32)
+
+    def hand_on(t):
+        arrived(sib_in.at[t], s_snd.at[t], s_rcv.at[t])
+        chip_out[t] = (acc[t, core] + sib_in[t].astype(F32)).astype(BF16)
+        go(send(chip_out.at[t], chip_in.at[t], x_snd.at[t], x_rcv.at[t], seq=2 * src_chip(t) + core))
+
+    order = list(range(1, nc)) + [0]
+    for pos, t in enumerate(order):
+        for g in range(groups):
+            w = s_scr[t, g] * norm[g]
+            ds = (w * (p_scr[t, g] - delta[g]) * scale).astype(BF16)
+            ds_scr[t, g] = ds
+            dk = jnp.dot(ds, q_st[g], preferred_element_type=F32)
+            dv = jnp.dot(w.astype(BF16), d_st[g], preferred_element_type=F32)
+            cols = slice(g * hd, (g + 1) * hd)
+            for i in range(2):
+                acc[t, i, 0, :, cols] = dk[i * tokens:(i + 1) * tokens]
+                acc[t, i, 1, :, cols] = dv[i * tokens:(i + 1) * tokens]
+            k_part = k_part + jnp.sum(dk * k_hat[t, g], axis=0, keepdims=True)
+        sib_out[t] = acc[t, 1 - core].astype(BF16)
+        go(send(sib_out.at[t], sib_in.at[t], s_snd.at[t], s_rcv.at[t], seq=sib))
+        if pos >= 1:
+            hand_on(order[pos - 1])
+
+    q_part = jnp.zeros((1, hd), F32)
+    for g in range(groups):
+        dq_tr = jnp.zeros((hd, wide), F32)
+        for t in range(nc):
+            dq_tr = dq_tr + jnp.dot(k_tr[t, g], ds_scr[t, g], preferred_element_type=F32)
+        for i in range(per):
+            h = g * per + i
+            dq = dq_tr[:, i * tokens:(i + 1) * tokens].T.astype(BF16).astype(F32)
+            x = q_hat[h]
+            q_part = q_part + jnp.sum(dq * x, axis=0, keepdims=True)
+            y = dq * q_gain
+            mean = jnp.mean(y * x, axis=1, keepdims=True)
+            q_res[:, h * hd:(h + 1) * hd] = (q_inv[h] * (y - x * mean)).astype(BF16)
+    out_q = local(q_res, q_out, 5)
+
+    part1[md] = jnp.concatenate([q_part, k_part, jnp.zeros((6, hd), F32)], axis=0)
+    for r in range(1, dpn):
+        go(send(part1.at[md], part1.at[md], p1_snd.at[r], p1_rcv.at[r], dp=lax.rem(md + r, dpn)))
+    arrived(sib_in.at[0], s_snd.at[0], s_rcv.at[0])
+    total = acc[0, core] + sib_in[0].astype(F32)
+    for r in range(1, dpn):
+        arrived(part1.at[lax.rem(md + dpn - r, dpn)], p1_snd.at[r], p1_rcv.at[r])
+    gains = part1[0]
+    for i in range(1, dpn):
+        gains = gains + part1[i]
+    part2[me] = gains
+    for r in range(1, n):
+        go(send(part2.at[me], part2.at[me], p2_snd.at[r], p2_rcv.at[r], seq=lax.rem(me + r, n)))
+
+    for t in range(1, nc):
+        arrived(chip_in.at[t], x_snd.at[t], x_rcv.at[t])
+        total = total + chip_in[t].astype(F32)
+    v_out[...] = total[1].astype(BF16)
+    dk_all = total[0].astype(BF16).astype(F32)
+    for g in range(groups):
+        cols = slice(g * hd, (g + 1) * hd)
+        x = k_all[me, :, cols].astype(F32)
+        inv = lax.rsqrt(jnp.mean(x * x, axis=1, keepdims=True) + EPSILON)
+        x = x * inv
+        y = dk_all[:, cols] * k_gain
+        mean = jnp.mean(y * x, axis=1, keepdims=True)
+        k_out[:, cols] = (inv * (y - x * mean)).astype(BF16)
+
+    for r in range(1, n):
+        arrived(part2.at[lax.rem(me + n - r, n)], p2_snd.at[r], p2_rcv.at[r])
+    gains = part2[0]
+    for i in range(1, n):
+        gains = gains + part2[i]
+    share = hd // dpn
+    mine = jnp.zeros((8, share), F32)
+    for i in range(dpn):
+        mine = mine + jnp.where(md == i, gains[:, i * share:(i + 1) * share], 0.0)
+    gq_out[...] = mine[0:1]
+    gk_out[...] = mine[1:2]
+
+    out_q.wait()
+    for copy in pending:
+        copy.wait_send()
+
+
+def scratch_list(n, dpn, tokens, hd, heads, groups, held, blocks, slots):
+    nc = n // 2
+    wide = heads // groups * tokens
+    vm = pltpu.VMEM
+    dma = pltpu.SemaphoreType.DMA
+    kvd = groups * hd
+    arrays = [
+        vm((tokens, heads * hd), BF16),
+        vm((tokens, heads * hd), BF16),
+        vm((n, tokens, kvd), BF16),
+        vm((n, tokens, kvd), BF16),
+        vm((n, held, blocks, slots), jnp.int32),
+        vm((heads, slots), jnp.int32),
+        vm((dpn, 1, hd // dpn), F32),
+        vm((dpn, 1, hd // dpn), F32),
+        vm((n, heads, tokens), F32),
+        vm((heads, tokens, hd), F32),
+        vm((heads, tokens, hd), F32),
+        vm((groups, wide, hd), BF16),
+        vm((groups, hd, wide), BF16),
+        vm((groups, wide, hd), BF16),
+        vm((groups, hd, wide), BF16),
+        vm((nc, groups, 2 * tokens, hd), F32),
+        vm((nc, groups, hd, 2 * tokens), BF16),
+        vm((nc, groups, 2 * tokens, wide), F32),
+        vm((nc, groups, 2 * tokens, wide), F32),
+        vm((nc, groups, 2 * tokens, wide), BF16),
+        vm((nc, 2, 2, tokens, kvd), F32),
+        vm((nc, 2, tokens, kvd), BF16),
+        vm((nc, 2, tokens, kvd), BF16),
+        vm((nc, 2, tokens, kvd), BF16),
+        vm((nc, 2, tokens, kvd), BF16),
+        vm((tokens, heads * hd), BF16),
+        vm((dpn, 8, hd), F32),
+        vm((n, 8, hd), F32),
+    ]
+    sems = [dma((7,))] + [dma((nc,))] * 8 + [dma((n,))] * 2 + [dma((dpn,))] * 4
+    sems += [dma((nc,))] * 4 + [dma((dpn,))] * 2 + [dma((n,))] * 2
+    return arrays, sems
+
+
+def shards(n, dpn, q_raw, k_raw, v_raw, q_gain, k_gain, key_blocks, d_context):
+    hd = q_gain.shape[0] * dpn
+    tokens = q_raw.shape[1]
+    heads = q_raw.shape[2] // hd
+    groups = k_raw.shape[2] // hd
+    held, blocks, slots = key_blocks.shape
+    arrays, sems = scratch_list(n, dpn, tokens, hd, heads, groups, held, blocks, slots)
+    room = sum(math.prod(a.shape) * jnp.dtype(a.dtype).itemsize for a in arrays)
+    fits = room < VMEM_ROOM - 16 * 1024 * 1024
+    if n % 2 or tokens != BLK or q_raw.shape[0] != 1 or not fits:
+        return shards_by_head(q_raw, k_raw, v_raw, q_gain, k_gain, key_blocks, d_context)
+    anywhere = pl.BlockSpec(memory_space=pl.ANY)
+    vmem = pl.BlockSpec(memory_space=pltpu.VMEM)
+    share = hd // dpn
+    kvd = groups * hd
+    q_grad, k_grad, v_grad, gq, gk = pl.pallas_call(
+        functools.partial(token_kernel, n, dpn),
+        out_shape=(
+            jax.ShapeDtypeStruct((tokens, heads * hd), BF16),
+            jax.ShapeDtypeStruct((tokens, kvd), BF16),
+            jax.ShapeDtypeStruct((tokens, kvd), BF16),
+            jax.ShapeDtypeStruct((1, share), F32),
+            jax.ShapeDtypeStruct((1, share), F32),
+        ),
+        in_specs=[anywhere] * 7,
+        out_specs=(anywhere, vmem, vmem, vmem, vmem),
+        scratch_shapes=arrays + sems,
+        compiler_params=pltpu.CompilerParams(
+            collective_id=0, has_side_effects=True, vmem_limit_bytes=VMEM_ROOM
+        ),
+    )(q_raw[0], k_raw[0], v_raw[0], q_gain[None], k_gain[None], key_blocks, d_context[0])
+    return (q_grad[None], k_grad[None], v_grad[None], gq[0], gk[0])
+
+
 def solution(mesh):
     placed = (
         P("dp", "seq", None),
@@ -221,7 +570,7 @@
         P("dp", "seq", None),
     )
     return jax.shard_map(
-        shards,
+        functools.partial(shards, mesh.shape["seq"], mesh.shape["dp"]),
         mesh=mesh,
         in_specs=placed,
         out_specs=(

time: 156 us -> 37.3 us (0.24); the launches traced: 154 us -> 37.1 us
  blocking collectives: 50.2 us -> 0 us
  Pallas kernels: 0 us -> 30.7 us
  matrix products: 26.9 us -> 0 us
  starting transfers between devices: 25.7 us -> 0 us
  waiting for transfers between devices: 19.8 us -> 0 us
  local copies, waits for them, and re-layouts: 20 us -> 5.7 us
  other arithmetic: 9.61 us -> 0 us
    psum x1 -> x0, blocking collectives: 36.8 us -> none  [shards(): q_total, k_total = lax.psum((q_part, k_part), ('seq', 'dp'))]
    pallas_call x0 -> x1, Pallas kernels: none -> 30.7 us  [shards(): pl.pallas_call(functools.partial(token_kernel, n, dpn), out_shape=(jax.Sh...]
    dot_general x12 -> x0, matrix products: 26.9 us -> none  [the longest x1 5.58 us: one_group(): jnp.einsum('gsn,gskd->nkd', one_hot, value_pieces, precision=top_precision)]
    all_to_all x7 -> x0, starting transfers between devices: 25.7 us -> none  [the longest x1 4.14 us: shards(): lax.all_to_all(d_context[0], 'seq', split_axis=1, concat_axis=0, tiled=True)]
    all_to_all x7 -> x0, waiting for transfers between devices: 19.8 us -> none  [the longest x1 6.83 us: shards(): lax.all_to_all(v_wide, 'seq', split_axis=1, concat_axis=0, tiled=True)]
    unnamed x1 -> x0, blocking collectives: 13.4 us -> none
    gather x5 -> x0, local copies, waits for them, and re-layouts: 4.13 us -> none  [the longest x4 2.16 us: one_group(): selected_keys = k_tiles[chosen]]
    unnamed x80 -> x16, local copies, waits for them, and re-layouts: 9.17 us -> 5.7 us
  transfers between devices with their start and end apart: 7 -> 0, of which waited for: 5 -> 0; matrix products, arithmetic and copies ran while one was open for 25% -> 0% of each run, Pallas kernels for 0% -> 0%
where the time goes in v1:
time: 37.3 us; the launch traced here: 37.1 us
  Pallas kernels  30.7 us (82%)
  local copies, waits for them, and re-layouts  5.7 us (15%)
  between operations  0.66 us (2%)
    pallas_call x1, Pallas kernels, shards(): pl.pallas_call(functools.partial(token_kernel, n, dpn), out_shape=(jax.Sh...  30.7 us
    unnamed x16, local copies, waits for them, and re-layouts  5.7 us

profile of v1, /device:TPU:0, one launch (start us, length us, event | category | flops | bytes accessed | tf_op | source)
XLA Modules:
  0.0 37.1 jit_solution(13237178551219006878)
XLA Ops:
  0.6 0.0 copy-start.2
  0.6 0.7 %copy-done.2 = s32[1,8,6]{1,0,2:T(1,128)S(1)} copy-done((s32[1,8,6]{1,0,2:T(1,128)S(1)}, s32[1,8,6]{1,0,2:T(1,128)}, u32[]{:S(2)}) %copy-start.2) | copy-done | bytes 216
  1.3 0.7 %copy.12.kb_in = s32[1,8,6]{2,1,0:T(8,128)} copy(s32[1,8,6]{1,0,2:T(1,128)S(1)} %copy-done.2) | data formatting | bytes 384 | tf_op args[5]
  2.0 30.7 %shard_map.110 = (bf16[128,1024]{1,0:T(8,128)(2,1)}, bf16[128,256]{1,0:T(8,128)(2,1)}, bf16[128,256]{1,0:T(8,128)(2,1)}, f32[1,32]{1,0:T(1,128)}, f32[1,32]{1,0:T(1,128)}) custom-call(bf16[128,1024]{1,0:T(8,128)(2,1)} %bitcast.11, bf16[128,256]{1,0:T(8,128)(2,1)} %bitcast.14, bf16[128,256]{1,0:T(8,128)(2,1)} %bitcast.15, f32[1,32]{1,0:T(1,128)} %bitcast.18, ...), custom_call_target="tpu_custom_call" | custom-call | tf_op jit(solution)/shard_map/pallas_call | solution.py:543
  32.7 0.0 copy-start.1
  32.7 1.7 %copy.18 = bf16[1,128,1024]{2,1,0:T(8,128)(2,1)} copy(bf16[1,128,1024]{2,1,0:T(8,128)(2,1)} %bitcast.13) | data formatting | bytes 524288
  34.4 0.0 copy-done.1
  34.4 0.0 copy-start
  34.4 0.6 %copy.19 = bf16[1,128,256]{2,1,0:T(8,128)(2,1)} copy(bf16[1,128,256]{2,1,0:T(8,128)(2,1)S(1)} %bitcast.17) | data formatting | bytes 131072
  35.1 0.2 copy-done
  35.3 0.0 copy-start.4
  35.3 0.6 %copy.20 = bf16[1,128,256]{2,1,0:T(8,128)(2,1)} copy(bf16[1,128,256]{2,1,0:T(8,128)(2,1)S(1)} %bitcast.16) | data formatting | bytes 131072
  35.9 0.0 copy-done.4
  35.9 0.0 copy-start.3
  35.9 0.5 %copy.21 = f32[32]{0:T(128)} copy(f32[32]{0:T(128)S(1)} %bitcast.21) | data formatting | bytes 256
  36.4 0.1 copy-done.3
  36.6 0.5 %copy.22 = f32[32]{0:T(128)} copy(f32[32]{0:T(128)S(1)} %bitcast.20) | data formatting | bytes 256
Async XLA Ops:
  0.6 0.7 %copy-start.2 = (s32[1,8,6]{1,0,2:T(1,128)S(1)}, s32[1,8,6]{1,0,2:T(1,128)}, u32[]{:S(2)}) copy-start(s32[1,8,6]{1,0,2:T(1,128)} %param.12) | copy-start | bytes 580
  32.7 1.7 %copy-start.1 = (bf16[128,256]{1,0:T(8,128)(2,1)S(1)}, bf16[128,256]{1,0:T(8,128)(2,1)}, u32[]{:S(2)}) copy-start(bf16[128,256]{1,0:T(8,128)(2,1)} %get-tuple-element.11) | copy-start | bytes 196612
  34.4 0.9 %copy-start = (bf16[128,256]{1,0:T(8,128)(2,1)S(1)}, bf16[128,256]{1,0:T(8,128)(2,1)}, u32[]{:S(2)}) copy-start(bf16[128,256]{1,0:T(8,128)(2,1)} %get-tuple-element.12) | copy-start | bytes 196612
  35.3 0.6 %copy-start.4 = (f32[1,32]{1,0:T(1,128)S(1)}, f32[1,32]{1,0:T(1,128)}, u32[]{:S(2)}) copy-start(f32[1,32]{1,0:T(1,128)} %get-tuple-element.13) | copy-start | bytes 388
  35.9 0.6 %copy-start.3 = (f32[1,32]{1,0:T(1,128)S(1)}, f32[1,32]{1,0:T(1,128)}, u32[]{:S(2)}) copy-start(f32[1,32]{1,0:T(1,128)} %get-tuple-element.14) | copy-start | bytes 388

commit v2 on v1

--- a/solution.py
+++ b/solution.py
@@ -226,7 +226,7 @@
     q_s, d_s, k_all, v_all, kb_all, kbm, gq_all, gk_all, bias,
     q_hat, q_inv, q_st, q_tr, d_st, d_tr, k_hat, k_tr,
     s_scr, p_scr, ds_scr, acc, sib_out, sib_in, chip_out, chip_in,
-    q_res, part1, part2,
+    part1, part2,
     loc, k_snd, k_rcv, v_snd, v_rcv, kf_snd, kf_rcv, vf_snd, vf_rcv,
     b_snd, b_rcv, gq_snd, gq_rcv, gk_snd, gk_rcv,
     s_snd, s_rcv, x_snd, x_rcv, p1_snd, p1_rcv, p2_snd, p2_rcv,
@@ -264,8 +264,11 @@
         copy.start()
         return copy
 
-    own_k = local(k_in, k_all.at[me], 0)
-    own_v = local(v_in, v_all.at[me], 1)
+    def cols_of(ref, g):
+        return ref.at[:, g * hd:(g + 1) * hd]
+
+    own_k = [local(cols_of(k_in, g), k_all.at[g, me], 7 + g) for g in range(groups)]
+    own_v = [local(cols_of(v_in, g), v_all.at[g, me], 7 + groups + g) for g in range(groups)]
     own_gq = local(gq_in, gq_all.at[md], 2)
     own_gk = local(gk_in, gk_all.at[md], 3)
     own_kb = local(kb_in, kb_all.at[me], 4)
@@ -289,14 +292,17 @@
         to = lax.rem(md + r, dpn)
         go(send(gq_in, gq_all.at[md], gq_snd.at[r], gq_rcv.at[r], dp=to))
         go(send(gk_in, gk_all.at[md], gk_snd.at[r], gk_rcv.at[r], dp=to))
-    for t in range(1, nc):
-        go(send(k_in, k_all.at[me], k_snd.at[t], k_rcv.at[t], seq=2 * dst_chip(t) + core))
-    go(send(k_in, k_all.at[me], k_snd.at[0], k_rcv.at[0], seq=sib))
-    for t in range(1, nc):
-        go(send(v_in, v_all.at[me], v_snd.at[t], v_rcv.at[t], seq=2 * dst_chip(t) + core))
-    go(send(v_in, v_all.at[me], v_snd.at[0], v_rcv.at[0], seq=sib))
+    def spread(g):
+        for ref, held_in, snd, rcv in ((k_in, k_all, k_snd, k_rcv), (v_in, v_all, v_snd, v_rcv)):
+            for t in range(1, nc):
+                go(send(cols_of(ref, g), held_in.at[g, me], snd.at[g, t], rcv.at[g, t], seq=2 * dst_chip(t) + core))
+            go(send(cols_of(ref, g), held_in.at[g, me], snd.at[g, 0], rcv.at[g, 0], seq=sib))
+
+    spread(0)
     for r in range(1, n):
         go(send(kb_in, kb_all.at[me], b_snd.at[r], b_rcv.at[r], seq=lax.rem(me + r, n)))
+    for g in range(1, groups):
+        spread(g)
 
     def arrived(ref, snd, rcv):
         send(ref, ref, snd, rcv, seq=sib).wait_recv()
@@ -309,6 +315,25 @@
         d_st[g, rows, :] = x
         d_tr[g, :, rows] = x.astype(F32).T.astype(BF16)
     own_q.wait()
+    for h in range(heads):
+        x = q_s[:, h * hd:(h + 1) * hd].astype(F32)
+        inv = lax.rsqrt(jnp.mean(x * x, axis=1, keepdims=True) + EPSILON)
+        inv = jnp.broadcast_to(inv, (tokens, hd))
+        q_inv[h] = inv
+        q_hat[h] = x * inv
+
+    def forward(g, t):
+        frm = 2 * src_chip(t) + core
+        for held_in, snd, rcv, f_snd, f_rcv in (
+            (k_all, k_snd, k_rcv, kf_snd, kf_rcv), (v_all, v_snd, v_rcv, vf_snd, vf_rcv),
+        ):
+            ref = held_in.at[g, frm]
+            arrived(ref, snd.at[g, t], rcv.at[g, t])
+            go(send(ref, ref, f_snd.at[g, t], f_rcv.at[g, t], seq=sib))
+
+    for t in range(1, nc):
+        forward(0, t)
+
     own_gq.wait()
     own_gk.wait()
     for r in range(1, dpn):
@@ -317,118 +342,107 @@
         arrived(gk_all.at[frm], gk_snd.at[r], gk_rcv.at[r])
     q_gain = jnp.concatenate([gq_all[i] for i in range(dpn)], axis=1)
     k_gain = jnp.concatenate([gk_all[i] for i in range(dpn)], axis=1)
-    for h in range(heads):
-        g, i = h // per, h % per
-        rows = slice(i * tokens, (i + 1) * tokens)
-        x = q_s[:, h * hd:(h + 1) * hd].astype(F32)
-        inv = lax.rsqrt(jnp.mean(x * x, axis=1, keepdims=True) + EPSILON)
-        inv = jnp.broadcast_to(inv, (tokens, hd))
-        x = x * inv
-        q_inv[h] = inv
-        q_hat[h] = x
-        x = x * q_gain
-        q_st[g, rows, :] = x.astype(BF16)
-        q_tr[g, :, rows] = x.T.astype(BF16)
-
+
+    def query_tiles(g):
+        for i in range(per):
+            rows = slice(i * tokens, (i + 1) * tokens)
+            x = q_hat[g * per + i] * q_gain
+            q_st[g, rows, :] = x.astype(BF16)
+            q_tr[g, :, rows] = x.T.astype(BF16)
+
+    query_tiles(0)
     own_kb.wait()
     for r in range(1, n):
         arrived(kb_all.at[lax.rem(me + n - r, n)], b_snd.at[r], b_rcv.at[r])
-    held = kb_all.shape[1]
+    held = kb_all.shape[2]
     for h in range(heads):
-        kbm[h:h + 1, :] = kb_all[h // held, h % held, pl.ds(me, 1), :]
-    named = kbm[...]
+        kbm[h] = kb_all[h // held, :, h % held, :].astype(F32)
+    lane = lax.broadcasted_iota(jnp.int32, kbm.shape, 2)
+    named = jnp.max(jnp.where(lane == me, kbm[...], -1.0), axis=2, keepdims=True)
     for j in range(n):
-        hit = jnp.where((named == j) | (me < GLOB), 0.0, -jnp.inf)
-        bias[j] = jnp.broadcast_to(jnp.max(hit, axis=1, keepdims=True), (heads, tokens))
-
-    def forward(t):
-        frm = 2 * src_chip(t) + core
-        arrived(k_all.at[frm], k_snd.at[t], k_rcv.at[t])
-        go(send(k_all.at[frm], k_all.at[frm], kf_snd.at[t], kf_rcv.at[t], seq=sib))
-        arrived(v_all.at[frm], v_snd.at[t], v_rcv.at[t])
-        go(send(v_all.at[frm], v_all.at[frm], vf_snd.at[t], vf_rcv.at[t], seq=sib))
-
-    peak = [jnp.full((1, wide), -jnp.inf, F32) for _ in range(groups)]
-
-    def pair(t):
+        hit = jnp.where((named == float(j)) | (me < GLOB), 0.0, -jnp.inf)
+        bias[j] = jnp.broadcast_to(jnp.max(hit, axis=1, keepdims=True), (heads, 1, tokens))
+
+    def pair(g, t, peak):
         at = src_chip(t)
         if t == 0:
-            own_k.wait()
-            arrived(k_all.at[sib], k_snd.at[0], k_rcv.at[0])
+            own_k[g].wait()
+            arrived(k_all.at[g, sib], k_snd.at[g, 0], k_rcv.at[g, 0])
         else:
-            arrived(k_all.at[2 * at + 1 - core], kf_snd.at[t], kf_rcv.at[t])
-        keys = k_all[pl.ds(2 * at, 2)].reshape(2 * tokens, groups * hd)
-        for g in range(groups):
-            x = keys[:, g * hd:(g + 1) * hd].astype(F32)
-            inv = lax.rsqrt(jnp.mean(x * x, axis=1, keepdims=True) + EPSILON)
-            x = x * inv
-            k_hat[t, g] = x
-            x = x * k_gain
-            k_tr[t, g] = x.T.astype(BF16)
-            s = jnp.dot(x.astype(BF16), q_tr[g], preferred_element_type=F32)
-            for i in range(2):
-                block = bias[2 * at + i]
-                line = jnp.concatenate([block[h:h + 1] for h in range(g * per, (g + 1) * per)], axis=1)
-                part = s[i * tokens:(i + 1) * tokens] + line
-                s_scr[t, g, i * tokens:(i + 1) * tokens, :] = part
-                peak[g] = jnp.maximum(peak[g], jnp.max(part, axis=0, keepdims=True))
+            arrived(k_all.at[g, 2 * at + 1 - core], kf_snd.at[g, t], kf_rcv.at[g, t])
+        x = k_all[g, pl.ds(2 * at, 2)].reshape(2 * tokens, hd).astype(F32)
+        inv = lax.rsqrt(jnp.mean(x * x, axis=1, keepdims=True) + EPSILON)
+        x = x * inv
+        k_hat[t, g] = x
+        x = x * k_gain
+        k_tr[t, g] = x.T.astype(BF16)
+        s = jnp.dot(x.astype(BF16), q_tr[g], preferred_element_type=F32)
+        for i in range(2):
+            line = jnp.concatenate([bias[2 * at + i, h] for h in range(g * per, (g + 1) * per)], axis=1)
+            part = s[i * tokens:(i + 1) * tokens] + line
+            s_scr[t, g, i * tokens:(i + 1) * tokens, :] = part
+            peak = jnp.maximum(peak, jnp.max(part, axis=0, keepdims=True))
         if t == 0:
-            own_v.wait()
-            arrived(v_all.at[sib], v_snd.at[0], v_rcv.at[0])
+            own_v[g].wait()
+            arrived(v_all.at[g, sib], v_snd.at[g, 0], v_rcv.at[g, 0])
         else:
-            arrived(v_all.at[2 * at + 1 - core], vf_snd.at[t], vf_rcv.at[t])
-        vals = v_all[pl.ds(2 * at, 2)].reshape(2 * tokens, groups * hd)
-        for g in range(groups):
-            p_scr[t, g] = jnp.dot(vals[:, g * hd:(g + 1) * hd], d_tr[g], preferred_element_type=F32)
-
-    for t in range(nc):
-        if t + 1 < nc:
-            forward(t + 1)
-        pair(t)
-
-    norm, delta = [], []
+            arrived(v_all.at[g, 2 * at + 1 - core], vf_snd.at[g, t], vf_rcv.at[g, t])
+        vals = v_all[g, pl.ds(2 * at, 2)].reshape(2 * tokens, hd)
+        p_scr[t, g] = jnp.dot(vals, d_tr[g], preferred_element_type=F32)
+        return peak
+
+    def hand_on(g, t):
+        arrived(sib_in.at[g, t], s_snd.at[g, t], s_rcv.at[g, t])
+        chip_out[g, t] = (acc[g, t, core] + sib_in[g, t].astype(F32)).astype(BF16)
+        go(send(chip_out.at[g, t], chip_in.at[g, t], x_snd.at[g, t], x_rcv.at[g, t], seq=2 * src_chip(t) + core))
+
+    k_part = jnp.zeros((1, hd), F32)
+    order = list(range(1, nc)) + [0]
+    waiting = []
     for g in range(groups):
+        peak = jnp.full((1, wide), -jnp.inf, F32)
+        for t in range(nc):
+            peak = pair(g, t, peak)
+            if t == 0:
+                while waiting:
+                    hand_on(*waiting.pop(0))
+        if g + 1 < groups:
+            for t in range(1, nc):
+                forward(g + 1, t)
+            query_tiles(g + 1)
         total = jnp.zeros((1, wide), F32)
         cross = jnp.zeros((1, wide), F32)
         for t in range(nc):
-            e = jnp.exp2((s_scr[t, g] - peak[g]) * raise_by)
+            e = jnp.exp2((s_scr[t, g] - peak) * raise_by)
             s_scr[t, g] = e
             total = total + jnp.sum(e, axis=0, keepdims=True)
             cross = cross + jnp.sum(e * p_scr[t, g], axis=0, keepdims=True)
-        inv = 1.0 / total
-        norm.append(inv)
-        delta.append(cross * inv)
-
-    k_part = jnp.zeros((1, hd), F32)
-
-    def hand_on(t):
-        arrived(sib_in.at[t], s_snd.at[t], s_rcv.at[t])
-        chip_out[t] = (acc[t, core] + sib_in[t].astype(F32)).astype(BF16)
-        go(send(chip_out.at[t], chip_in.at[t], x_snd.at[t], x_rcv.at[t], seq=2 * src_chip(t) + core))
-
-    order = list(range(1, nc)) + [0]
-    for pos, t in enumerate(order):
-        for g in range(groups):
-            w = s_scr[t, g] * norm[g]
-            ds = (w * (p_scr[t, g] - delta[g]) * scale).astype(BF16)
+        norm = 1.0 / total
+        delta = cross * norm
+        for t in order:
+            w = s_scr[t, g] * norm
+            ds = (w * (p_scr[t, g] - delta) * scale).astype(BF16)
             ds_scr[t, g] = ds
             dk = jnp.dot(ds, q_st[g], preferred_element_type=F32)
             dv = jnp.dot(w.astype(BF16), d_st[g], preferred_element_type=F32)
-            cols = slice(g * hd, (g + 1) * hd)
             for i in range(2):
-                acc[t, i, 0, :, cols] = dk[i * tokens:(i + 1) * tokens]
-                acc[t, i, 1, :, cols] = dv[i * tokens:(i + 1) * tokens]
+                acc[g, t, i, 0] = dk[i * tokens:(i + 1) * tokens]
+                acc[g, t, i, 1] = dv[i * tokens:(i + 1) * tokens]
             k_part = k_part + jnp.sum(dk * k_hat[t, g], axis=0, keepdims=True)
-        sib_out[t] = acc[t, 1 - core].astype(BF16)
-        go(send(sib_out.at[t], sib_in.at[t], s_snd.at[t], s_rcv.at[t], seq=sib))
-        if pos >= 1:
-            hand_on(order[pos - 1])
+            sib_out[g, t] = acc[g, t, 1 - core].astype(BF16)
+            go(send(sib_out.at[g, t], sib_in.at[g, t], s_snd.at[g, t], s_rcv.at[g, t], seq=sib))
+            if waiting:
+                hand_on(*waiting.pop(0))
+            if t != 0:
+                waiting.append((g, t))
 
     q_part = jnp.zeros((1, hd), F32)
     for g in range(groups):
         dq_tr = jnp.zeros((hd, wide), F32)
         for t in range(nc):
             dq_tr = dq_tr + jnp.dot(k_tr[t, g], ds_scr[t, g], preferred_element_type=F32)
+        while waiting:
+            hand_on(*waiting.pop(0))
         for i in range(per):
             h = g * per + i
             dq = dq_tr[:, i * tokens:(i + 1) * tokens].T.astype(BF16).astype(F32)
@@ -436,14 +450,15 @@
             q_part = q_part + jnp.sum(dq * x, axis=0, keepdims=True)
             y = dq * q_gain
             mean = jnp.mean(y * x, axis=1, keepdims=True)
-            q_res[:, h * hd:(h + 1) * hd] = (q_inv[h] * (y - x * mean)).astype(BF16)
-    out_q = local(q_res, q_out, 5)
+            q_out[:, h * hd:(h + 1) * hd] = (q_inv[h] * (y - x * mean)).astype(BF16)
 
     part1[md] = jnp.concatenate([q_part, k_part, jnp.zeros((6, hd), F32)], axis=0)
     for r in range(1, dpn):
         go(send(part1.at[md], part1.at[md], p1_snd.at[r], p1_rcv.at[r], dp=lax.rem(md + r, dpn)))
-    arrived(sib_in.at[0], s_snd.at[0], s_rcv.at[0])
-    total = acc[0, core] + sib_in[0].astype(F32)
+    totals = []
+    for g in range(groups):
+        arrived(sib_in.at[g, 0], s_snd.at[g, 0], s_rcv.at[g, 0])
+        totals.append(acc[g, 0, core] + sib_in[g, 0].astype(F32))
     for r in range(1, dpn):
         arrived(part1.at[lax.rem(md + dpn - r, dpn)], p1_snd.at[r], p1_rcv.at[r])
     gains = part1[0]
@@ -453,17 +468,17 @@
     for r in range(1, n):
         go(send(part2.at[me], part2.at[me], p2_snd.at[r], p2_rcv.at[r], seq=lax.rem(me + r, n)))
 
-    for t in range(1, nc):
-        arrived(chip_in.at[t], x_snd.at[t], x_rcv.at[t])
-        total = total + chip_in[t].astype(F32)
-    v_out[...] = total[1].astype(BF16)
-    dk_all = total[0].astype(BF16).astype(F32)
     for g in range(groups):
+        total = totals[g]
+        for t in range(1, nc):
+            arrived(chip_in.at[g, t], x_snd.at[g, t], x_rcv.at[g, t])
+            total = total + chip_in[g, t].astype(F32)
         cols = slice(g * hd, (g + 1) * hd)
-        x = k_all[me, :, cols].astype(F32)
+        v_out[:, cols] = total[1].astype(BF16)
+        x = k_all[g, me].astype(F32)
         inv = lax.rsqrt(jnp.mean(x * x, axis=1, keepdims=True) + EPSILON)
         x = x * inv
-        y = dk_all[:, cols] * k_gain
+        y = total[0].astype(BF16).astype(F32) * k_gain
         mean = jnp.mean(y * x, axis=1, keepdims=True)
         k_out[:, cols] = (inv * (y - x * mean)).astype(BF16)
 
@@ -479,9 +494,17 @@
     gq_out[...] = mine[0:1]
     gk_out[...] = mine[1:2]
 
-    out_q.wait()
     for copy in pending:
         copy.wait_send()
+
+
+def store_kernel(*refs):
+    sems = refs[10]
+    copies = [pltpu.make_async_copy(refs[i], refs[5 + i], sems.at[i]) for i in range(5)]
+    for copy in copies:
+        copy.start()
+    for copy in copies:
+        copy.wait()
 
 
 def scratch_list(n, dpn, tokens, hd, heads, groups, held, blocks, slots):
@@ -489,17 +512,16 @@
     wide = heads // groups * tokens
     vm = pltpu.VMEM
     dma = pltpu.SemaphoreType.DMA
-    kvd = groups * hd
     arrays = [
         vm((tokens, heads * hd), BF16),
         vm((tokens, heads * hd), BF16),
-        vm((n, tokens, kvd), BF16),
-        vm((n, tokens, kvd), BF16),
-        vm((n, held, blocks, slots), jnp.int32),
-        vm((heads, slots), jnp.int32),
+        vm((groups, n, tokens, hd), BF16),
+        vm((groups, n, tokens, hd), BF16),
+        vm((n, slots, held, blocks), jnp.int32),
+        vm((heads, slots, blocks), F32),
         vm((dpn, 1, hd // dpn), F32),
         vm((dpn, 1, hd // dpn), F32),
-        vm((n, heads, tokens), F32),
+        vm((n, heads, 1, tokens), F32),
         vm((heads, tokens, hd), F32),
         vm((heads, tokens, hd), F32),
         vm((groups, wide, hd), BF16),
@@ -511,17 +533,16 @@
         vm((nc, groups, 2 * tokens, wide), F32),
         vm((nc, groups, 2 * tokens, wide), F32),
         vm((nc, groups, 2 * tokens, wide), BF16),
-        vm((nc, 2, 2, tokens, kvd), F32),
-        vm((nc, 2, tokens, kvd), BF16),
-        vm((nc, 2, tokens, kvd), BF16),
-        vm((nc, 2, tokens, kvd), BF16),
-        vm((nc, 2, tokens, kvd), BF16),
-        vm((tokens, heads * hd), BF16),
+        vm((groups, nc, 2, 2, tokens, hd), F32),
+        vm((groups, nc, 2, tokens, hd), BF16),
+        vm((groups, nc, 2, tokens, hd), BF16),
+        vm((groups, nc, 2, tokens, hd), BF16),
+        vm((groups, nc, 2, tokens, hd), BF16),
         vm((dpn, 8, hd), F32),
         vm((n, 8, hd), F32),
     ]
-    sems = [dma((7,))] + [dma((nc,))] * 8 + [dma((n,))] * 2 + [dma((dpn,))] * 4
-    sems += [dma((nc,))] * 4 + [dma((dpn,))] * 2 + [dma((n,))] * 2
+    sems = [dma((7 + 2 * groups,))] + [dma((groups, nc))] * 8 + [dma((n,))] * 2 + [dma((dpn,))] * 4
+    sems += [dma((groups, nc))] * 4 + [dma((dpn,))] * 2 + [dma((n,))] * 2
     return arrays, sems
 
 
@@ -543,20 +564,29 @@
     q_grad, k_grad, v_grad, gq, gk = pl.pallas_call(
         functools.partial(token_kernel, n, dpn),
         out_shape=(
-            jax.ShapeDtypeStruct((tokens, heads * hd), BF16),
-            jax.ShapeDtypeStruct((tokens, kvd), BF16),
-            jax.ShapeDtypeStruct((tokens, kvd), BF16),
-            jax.ShapeDtypeStruct((1, share), F32),
-            jax.ShapeDtypeStruct((1, share), F32),
+            pltpu.VMEM((tokens, heads * hd), BF16),
+            pltpu.VMEM((tokens, kvd), BF16),
+            pltpu.VMEM((tokens, kvd), BF16),
+            pltpu.VMEM((1, share), F32),
+            pltpu.VMEM((1, share), F32),
         ),
         in_specs=[anywhere] * 7,
-        out_specs=(anywhere, vmem, vmem, vmem, vmem),
+        out_specs=(vmem,) * 5,
         scratch_shapes=arrays + sems,
         compiler_params=pltpu.CompilerParams(
             collective_id=0, has_side_effects=True, vmem_limit_bytes=VMEM_ROOM
         ),
-    )(q_raw[0], k_raw[0], v_raw[0], q_gain[None], k_gain[None], key_blocks, d_context[0])
-    return (q_grad[None], k_grad[None], v_grad[None], gq[0], gk[0])
+    )(q_raw[0], k_raw[0], v_raw[0], q_gain[None], k_gain[None], key_blocks.transpose(2, 0, 1), d_context[0])
+    done = (q_grad, k_grad, v_grad, gq, gk)
+    done = pl.pallas_call(
+        store_kernel,
+        out_shape=tuple(jax.ShapeDtypeStruct(x.shape, x.dtype) for x in done),
+        in_specs=[vmem] * 5,
+        out_specs=(anywhere,) * 5,
+        scratch_shapes=[pltpu.SemaphoreType.DMA((5,))],
+        compiler_params=pltpu.CompilerParams(vmem_limit_bytes=4 * 1024 * 1024),
+    )(*done)
+    return (done[0][None], done[1][None], done[2][None], done[3][0], done[4][0])
 
 
 def solution(mesh):

time: 37.3 us -> 32.8 us (0.88)
  local copies, waits for them, and re-layouts: 5.7 us -> 0 us
  Pallas kernels: 30.7 us -> 32 us
    unnamed x16 -> x0, local copies, waits for them, and re-layouts: 5.7 us -> none
    pallas_call x1 -> x2, Pallas kernels: 30.7 us -> 32 us  [the longest x1 31.3 us: shards(): pl.pallas_call(functools.partial(token_kernel, n, dpn), out_shape=(pltpu....]
where the time goes in v2:
time: 32.8 us; the launch traced here: 32.7 us
  Pallas kernels  32 us (98%)
  between operations  0.64 us (2%)
    pallas_call x1, Pallas kernels, shards(): pl.pallas_call(functools.partial(token_kernel, n, dpn), out_shape=(pltpu....  31.3 us
    pallas_call x1, Pallas kernels, shards(): pl.pallas_call(store_kernel, out_shape=tuple((jax.ShapeDtypeStruct(x.shap...  0.79 us

profile of v2, /device:TPU:0, one launch (start us, length us, event | category | flops | bytes accessed | tf_op | source)
XLA Modules:
  0.0 32.7 jit_solution(18358613754029082398)
XLA Ops:
  0.6 31.3 %shard_map.110 = (bf16[128,1024]{1,0:T(8,128)(2,1)S(1)}, bf16[128,256]{1,0:T(8,128)(2,1)S(1)}, bf16[128,256]{1,0:T(8,128)(2,1)S(1)}, f32[1,32]{1,0:T(1,128)S(1)}, f32[1,32]{1,0:T(1,128)S(1)}) custom-call(bf16[128,1024]{1,0:T(8,128)(2,1)} %bitcast.12, bf16[128,256]{1,0:T(8,128)(2,1)} %bitcast.14, bf16[128,256]{1,0:T(8,128)(2,1)} %bitcast.15, ...), custom_call_target="tpu_custom_call" | custom-call | tf_op jit(solution)/shard_map/pallas_call | solution.py:564
  31.9 0.8 %shard_map.111 = (bf16[128,1024]{1,0:T(8,128)(2,1)}, bf16[128,256]{1,0:T(8,128)(2,1)}, bf16[128,256]{1,0:T(8,128)(2,1)}, f32[1,32]{1,0:T(1,128)}, f32[1,32]{1,0:T(1,128)}) custom-call(bf16[128,1024]{1,0:T(8,128)(2,1)S(1)} %get-tuple-element.15.refs_0_, bf16[128,256]{1,0:T(8,128)(2,1)S(1)} %get-tuple-element.16.refs_1_, ...), custom_call_target="tpu_custom_call" | custom-call | tf_op jit(solution)/shard_map/pallas_call | solution.py:581

commit v3 on v2

--- a/solution.py
+++ b/solution.py
@@ -216,7 +216,12 @@
 F32 = jnp.float32
 BF16 = jnp.bfloat16
 MESH = pl.DeviceIdType.MESH
+CHUNK = 32
 VMEM_ROOM = 56 * 1024 * 1024
+
+
+def fold_rows(tile):
+    return jnp.sum(tile.reshape(tile.shape[0] // 8, 8, tile.shape[1]), axis=0)
 
 
 def token_kernel(
@@ -225,7 +230,7 @@
     q_out, k_out, v_out, gq_out, gk_out,
     q_s, d_s, k_all, v_all, kb_all, kbm, gq_all, gk_all, bias,
     q_hat, q_inv, q_st, q_tr, d_st, d_tr, k_hat, k_tr,
-    s_scr, p_scr, ds_scr, acc, sib_out, sib_in, chip_out, chip_in,
+    s_scr, p_scr, ds_scr, w_scr, acc, sib_out, sib_in, chip_out, chip_in,
     part1, part2,
     loc, k_snd, k_rcv, v_snd, v_rcv, kf_snd, kf_rcv, vf_snd, vf_rcv,
     b_snd, b_rcv, gq_snd, gq_rcv, gk_snd, gk_rcv,
@@ -280,6 +285,13 @@
         pl.semaphore_signal(barrier, inc=1, device_id={"seq": lax.rem(me + r, n)}, device_id_type=MESH)
     for r in range(1, dpn):
         pl.semaphore_signal(barrier, inc=1, device_id={"dp": lax.rem(md + r, dpn)}, device_id_type=MESH)
+    own_d.wait()
+    for h in range(heads):
+        g, i = h // per, h % per
+        rows = slice(i * tokens, (i + 1) * tokens)
+        x = d_s[:, h * hd:(h + 1) * hd]
+        d_st[g, rows, :] = x
+        d_tr[g, :, rows] = x.astype(F32).T.astype(BF16)
     pl.semaphore_wait(barrier, n - 1 + dpn - 1)
 
     pending = []
@@ -307,13 +319,6 @@
     def arrived(ref, snd, rcv):
         send(ref, ref, snd, rcv, seq=sib).wait_recv()
 
-    own_d.wait()
-    for h in range(heads):
-        g, i = h // per, h % per
-        rows = slice(i * tokens, (i + 1) * tokens)
-        x = d_s[:, h * hd:(h + 1) * hd]
-        d_st[g, rows, :] = x
-        d_tr[g, :, rows] = x.astype(F32).T.astype(BF16)
     own_q.wait()
     for h in range(heads):
         x = q_s[:, h * hd:(h + 1) * hd].astype(F32)
@@ -330,9 +335,6 @@
             ref = held_in.at[g, frm]
             arrived(ref, snd.at[g, t], rcv.at[g, t])
             go(send(ref, ref, f_snd.at[g, t], f_rcv.at[g, t], seq=sib))
-
-    for t in range(1, nc):
-        forward(0, t)
 
     own_gq.wait()
     own_gk.wait()
@@ -362,6 +364,9 @@
     for j in range(n):
         hit = jnp.where((named == float(j)) | (me < GLOB), 0.0, -jnp.inf)
         bias[j] = jnp.broadcast_to(jnp.max(hit, axis=1, keepdims=True), (heads, 1, tokens))
+
+    for t in range(1, nc):
+        forward(0, t)
 
     def pair(g, t, peak):
         at = src_chip(t)
@@ -381,7 +386,7 @@
             line = jnp.concatenate([bias[2 * at + i, h] for h in range(g * per, (g + 1) * per)], axis=1)
             part = s[i * tokens:(i + 1) * tokens] + line
             s_scr[t, g, i * tokens:(i + 1) * tokens, :] = part
-            peak = jnp.maximum(peak, jnp.max(part, axis=0, keepdims=True))
+            peak = jnp.maximum(peak, jnp.max(part.reshape(tokens // 8, 8, wide), axis=0))
         if t == 0:
             own_v[g].wait()
             arrived(v_all.at[g, sib], v_snd.at[g, 0], v_rcv.at[g, 0])
@@ -400,7 +405,7 @@
     order = list(range(1, nc)) + [0]
     waiting = []
     for g in range(groups):
-        peak = jnp.full((1, wide), -jnp.inf, F32)
+        peak = jnp.full((8, wide), -jnp.inf, F32)
         for t in range(nc):
             peak = pair(g, t, peak)
             if t == 0:
@@ -410,21 +415,28 @@
             for t in range(1, nc):
                 forward(g + 1, t)
             query_tiles(g + 1)
-        total = jnp.zeros((1, wide), F32)
-        cross = jnp.zeros((1, wide), F32)
+        peak = jnp.max(peak, axis=0, keepdims=True)
+        total = jnp.zeros((8, wide), F32)
+        cross = jnp.zeros((8, wide), F32)
         for t in range(nc):
-            e = jnp.exp2((s_scr[t, g] - peak) * raise_by)
-            s_scr[t, g] = e
-            total = total + jnp.sum(e, axis=0, keepdims=True)
-            cross = cross + jnp.sum(e * p_scr[t, g], axis=0, keepdims=True)
+            for r in range(0, 2 * tokens, CHUNK):
+                rows = slice(r, r + CHUNK)
+                e = jnp.exp2((s_scr[t, g, rows, :] - peak) * raise_by)
+                s_scr[t, g, rows, :] = e
+                total = total + fold_rows(e)
+                cross = cross + fold_rows(e * p_scr[t, g, rows, :])
+        total = jnp.sum(total, axis=0, keepdims=True)
+        cross = jnp.sum(cross, axis=0, keepdims=True)
         norm = 1.0 / total
         delta = cross * norm
         for t in order:
-            w = s_scr[t, g] * norm
-            ds = (w * (p_scr[t, g] - delta) * scale).astype(BF16)
-            ds_scr[t, g] = ds
-            dk = jnp.dot(ds, q_st[g], preferred_element_type=F32)
-            dv = jnp.dot(w.astype(BF16), d_st[g], preferred_element_type=F32)
+            for r in range(0, 2 * tokens, CHUNK):
+                rows = slice(r, r + CHUNK)
+                w = s_scr[t, g, rows, :] * norm
+                w_scr[t, rows, :] = w.astype(BF16)
+                ds_scr[t, g, rows, :] = (w * ((p_scr[t, g, rows, :] - delta) * scale)).astype(BF16)
+            dk = jnp.dot(ds_scr[t, g], q_st[g], preferred_element_type=F32)
+            dv = jnp.dot(w_scr[t], d_st[g], preferred_element_type=F32)
             for i in range(2):
                 acc[g, t, i, 0] = dk[i * tokens:(i + 1) * tokens]
                 acc[g, t, i, 1] = dv[i * tokens:(i + 1) * tokens]
@@ -436,7 +448,10 @@
             if t != 0:
                 waiting.append((g, t))
 
-    q_part = jnp.zeros((1, hd), F32)
+    q_part = k_part * k_gain / q_gain
+    part1[md] = jnp.concatenate([q_part, k_part, jnp.zeros((6, hd), F32)], axis=0)
+    for r in range(1, dpn):
+        go(send(part1.at[md], part1.at[md], p1_snd.at[r], p1_rcv.at[r], dp=lax.rem(md + r, dpn)))
     for g in range(groups):
         dq_tr = jnp.zeros((hd, wide), F32)
         for t in range(nc):
@@ -447,27 +462,23 @@
             h = g * per + i
             dq = dq_tr[:, i * tokens:(i + 1) * tokens].T.astype(BF16).astype(F32)
             x = q_hat[h]
-            q_part = q_part + jnp.sum(dq * x, axis=0, keepdims=True)
             y = dq * q_gain
             mean = jnp.mean(y * x, axis=1, keepdims=True)
             q_out[:, h * hd:(h + 1) * hd] = (q_inv[h] * (y - x * mean)).astype(BF16)
-
-    part1[md] = jnp.concatenate([q_part, k_part, jnp.zeros((6, hd), F32)], axis=0)
-    for r in range(1, dpn):
-        go(send(part1.at[md], part1.at[md], p1_snd.at[r], p1_rcv.at[r], dp=lax.rem(md + r, dpn)))
+        if g == 0:
+            for r in range(1, dpn):
+                arrived(part1.at[lax.rem(md + dpn - r, dpn)], p1_snd.at[r], p1_rcv.at[r])
+            gains = part1[0]
+            for i in range(1, dpn):
+                gains = gains + part1[i]
+            part2[me] = gains
+            for r in range(1, n):
+                go(send(part2.at[me], part2.at[me], p2_snd.at[r], p2_rcv.at[r], seq=lax.rem(me + r, n)))
+
     totals = []
     for g in range(groups):
         arrived(sib_in.at[g, 0], s_snd.at[g, 0], s_rcv.at[g, 0])
         totals.append(acc[g, 0, core] + sib_in[g, 0].astype(F32))
-    for r in range(1, dpn):
-        arrived(part1.at[lax.rem(md + dpn - r, dpn)], p1_snd.at[r], p1_rcv.at[r])
-    gains = part1[0]
-    for i in range(1, dpn):
-        gains = gains + part1[i]
-    part2[me] = gains
-    for r in range(1, n):
-        go(send(part2.at[me], part2.at[me], p2_snd.at[r], p2_rcv.at[r], seq=lax.rem(me + r, n)))
-
     for g in range(groups):
         total = totals[g]
         for t in range(1, nc):
@@ -533,6 +544,7 @@
         vm((nc, groups, 2 * tokens, wide), F32),
         vm((nc, groups, 2 * tokens, wide), F32),
         vm((nc, groups, 2 * tokens, wide), BF16),
+        vm((nc, 2 * tokens, wide), BF16),
         vm((groups, nc, 2, 2, tokens, hd), F32),
         vm((groups, nc, 2, tokens, hd), BF16),
         vm((groups, nc, 2, tokens, hd), BF16),

time: 32.8 us -> 32.9 us (level)
  no operation moved by 1% of the time
where the time goes in v3:
time: 32.9 us; the launch traced here: 32.8 us
  Pallas kernels  32.1 us (98%)
  between operations  0.64 us (2%)
    pallas_call x1, Pallas kernels, shards(): pl.pallas_call(functools.partial(token_kernel, n, dpn), out_shape=(pltpu....  31.3 us
    pallas_call x1, Pallas kernels, shards(): pl.pallas_call(store_kernel, out_shape=tuple((jax.ShapeDtypeStruct(x.shap...  0.79 us

profile of v3, /device:TPU:0, one launch (start us, length us, event | category | flops | bytes accessed | tf_op | source)
XLA Modules:
  0.0 32.8 jit_solution(8335389940229735738)
XLA Ops:
  0.6 31.3 %shard_map.110 = (bf16[128,1024]{1,0:T(8,128)(2,1)S(1)}, bf16[128,256]{1,0:T(8,128)(2,1)S(1)}, bf16[128,256]{1,0:T(8,128)(2,1)S(1)}, f32[1,32]{1,0:T(1,128)S(1)}, f32[1,32]{1,0:T(1,128)S(1)}) custom-call(bf16[128,1024]{1,0:T(8,128)(2,1)} %bitcast.12, bf16[128,256]{1,0:T(8,128)(2,1)} %bitcast.14, bf16[128,256]{1,0:T(8,128)(2,1)} %bitcast.15, ...), custom_call_target="tpu_custom_call" | custom-call | tf_op jit(solution)/shard_map/pallas_call | solution.py:576
  32.0 0.8 %shard_map.111 = (bf16[128,1024]{1,0:T(8,128)(2,1)}, bf16[128,256]{1,0:T(8,128)(2,1)}, bf16[128,256]{1,0:T(8,128)(2,1)}, f32[1,32]{1,0:T(1,128)}, f32[1,32]{1,0:T(1,128)}) custom-call(bf16[128,1024]{1,0:T(8,128)(2,1)S(1)} %get-tuple-element.15.refs_0_, bf16[128,256]{1,0:T(8,128)(2,1)S(1)} %get-tuple-element.16.refs_1_, ...), custom_call_target="tpu_custom_call" | custom-call | tf_op jit(solution)/shard_map/pallas_call | solution.py:593
